TPU v7x, 32 devices: a whole 2x2x4 slice. The times are simulated.
32 devices in a mesh: row: 8 (over y, x, core), col: 4 (over z).
Axes of the slice: x: 2, y: 2, z: 4, core: 2. Of those that a mesh axis runs over, the one named last changes fastest.
Arguments:
- object_field: float32 [2, 4096, 2048], P(None, 'row', 'col'), may hold values from -6 to 6
- illumination: float32 [2, 256, 256], replicated, may hold values from -6 to 6
- amplitude: bfloat16 [512, 256, 256], P(('row', 'col')), may hold values from 0 to 2
- offsets: int32 [512, 2], P(('row', 'col')), may hold values from 0 to 3840, as said below
- slot_counts: int32 [32], replicated, may hold values from 1 to 16, 256 in all
Outputs:
- object_gradient: float32 [2, 4096, 2048], P(None, 'row', 'col')
- probe_gradient: float32 [2, 256, 256], replicated
Inputs may be any that keep to these rules, and one draw needn't show every extreme that they name: `offsets`: slot j belongs to region d = j // 16, with row index d // 4 and column index d mod 4 (region (r, c)); its row offset lies in [r * 512, (r + 1) * 512) and its column offset in [c * 512, (c + 1) * 512), and every patch lies inside the object. Region d's live slots are its first slot_counts[d]; all counts sum to 256 and some region is full.
All inputs are finite; a program needn't handle non-finite values.
Results may differ from a plain program's by a relative error of at most 0.0045.
Values sent between devices are 32-bit elements; how exact they have to be, the bound alone decides.
No kernel may reach another device: no remote copies, remote signals or barrier semaphores. Data moves between devices by JAX's collectives and lax.ppermute only.
A program may use at most 128 MiB of HBM per device.

v0:
```python
import math

import jax
import jax.numpy as jnp
from jax import lax
from jax.sharding import PartitionSpec as P


def shifted(value, axis, steps):
    count = lax.axis_size(axis)
    leading, last = (max(0, -steps), min(count, count - steps))
    return lax.ppermute(value, axis, [(source, source + steps) for source in range(leading, last)])


def dft_tables(window, direction):
    positions = jnp.arange(window, dtype=jnp.int32)
    product = positions[:, None] * positions[None, :] % window
    angle = product.astype(jnp.float32) * (2.0 * math.pi / window)
    factor = 1.0 / math.sqrt(window)
    cosine = jnp.cos(angle) * factor
    sine = direction * jnp.sin(angle) * factor
    left = jnp.stack([jnp.stack([cosine, -sine]), jnp.stack([sine, cosine])]).astype(jnp.bfloat16)
    right = jnp.stack([jnp.stack([cosine, sine]), jnp.stack([-sine, cosine])]).astype(jnp.bfloat16)
    return (left, right)


def transform(field, tables):
    left, right = tables
    half = jnp.einsum("oiab,nibd->noad", left, field, preferred_element_type=jnp.float32).astype(
        jnp.bfloat16
    )
    return jnp.einsum("niab,iobd->noad", half, right, preferred_element_type=jnp.float32)


def gradient_block(patches, amplitudes, illumination, forward, inverse):
    real_probe = illumination[0]
    imag_probe = illumination[1]
    exit_real = real_probe * patches[:, 0] - imag_probe * patches[:, 1]
    exit_imag = real_probe * patches[:, 1] + imag_probe * patches[:, 0]
    exit_wave = jnp.stack([exit_real, exit_imag], axis=1).astype(jnp.bfloat16)
    far_field = transform(exit_wave, forward)
    magnitude = jnp.sqrt(far_field[:, 0] ** 2 + far_field[:, 1] ** 2 + 0.25)
    factor = 1.0 - amplitudes.astype(jnp.float32) / magnitude
    residual = (far_field * factor[:, None]).astype(jnp.bfloat16)
    back_field = transform(residual, inverse)
    object_terms = jnp.stack(
        [
            real_probe * back_field[:, 0] + imag_probe * back_field[:, 1],
            real_probe * back_field[:, 1] - imag_probe * back_field[:, 0],
        ],
        axis=1,
    )
    probe_terms = jnp.stack(
        [
            patches[:, 0] * back_field[:, 0] + patches[:, 1] * back_field[:, 1],
            patches[:, 0] * back_field[:, 1] - patches[:, 1] * back_field[:, 0],
        ],
        axis=1,
    )
    return (object_terms, probe_terms)


def shift_table(remainder, window, lane):
    source = jnp.arange(window + lane, dtype=jnp.int32)
    target = jnp.arange(window, dtype=jnp.int32)
    return (source[:, None] == target[None, :] + remainder).astype(jnp.float32)


def fetch_patch(extended, corner_row, corner_col, window, lane):
    zero_index = jnp.zeros((), jnp.int32)
    aligned = corner_col // lane * lane
    remainder = corner_col - aligned
    block = lax.dynamic_slice(
        extended, (zero_index, corner_row, aligned), (2, window, window + lane)
    )
    table = shift_table(remainder, window, lane)
    return jnp.einsum("crk,kw->crw", block, table, precision=lax.Precision.HIGHEST)


def add_patch(current, terms, corner_row, corner_col, window, lane):
    zero_index = jnp.zeros((), jnp.int32)
    aligned = corner_col // lane * lane
    remainder = corner_col - aligned
    table = shift_table(remainder, window, lane)
    spread = jnp.einsum("crw,kw->crk", terms, table, precision=lax.Precision.HIGHEST)
    block = lax.dynamic_slice(
        current, (zero_index, corner_row, aligned), (2, window, window + lane)
    )
    return lax.dynamic_update_slice(current, block + spread, (zero_index, corner_row, aligned))


def per_device(object_field, illumination, amplitude, offsets, slot_counts):
    tile_rows = object_field.shape[1]
    tile_cols = object_field.shape[2]
    window = illumination.shape[1]
    slots = offsets.shape[0]
    lane = math.gcd(128, tile_cols)
    right_strip = shifted(object_field[:, :, :window], "col", -1)
    widened = jnp.concatenate([object_field, right_strip], axis=2)
    lower_strip = shifted(widened[:, :window, :], "row", -1)
    extended = jnp.concatenate([widened, lower_strip], axis=1)
    row_index = lax.axis_index("row")
    col_index = lax.axis_index("col")
    anchor = jnp.stack([row_index * tile_rows, col_index * tile_cols])
    local_offsets = offsets - anchor[None, :]
    live_count = slot_counts[row_index * lax.axis_size("col") + col_index]
    forward = dft_tables(window, -1.0)
    inverse = dft_tables(window, 1.0)
    accumulated = jnp.zeros((2, tile_rows + window, tile_cols + window), jnp.float32)
    patches = jax.vmap(lambda corner: fetch_patch(extended, corner[0], corner[1], window, lane))(
        local_offsets
    )
    live_mask = (jnp.arange(slots, dtype=jnp.int32) < live_count).astype(jnp.float32)
    object_terms, probe_terms = gradient_block(patches, amplitude, illumination, forward, inverse)
    object_terms = object_terms * live_mask[:, None, None, None]
    probe_total = jnp.sum(probe_terms * live_mask[:, None, None, None], axis=0)

    def add_slot(slot_index, current):
        return add_patch(
            current,
            object_terms[slot_index],
            local_offsets[slot_index, 0],
            local_offsets[slot_index, 1],
            window,
            lane,
        )

    accumulated = lax.fori_loop(0, slots, add_slot, accumulated)
    lower_back = shifted(accumulated[:, tile_rows:, :], "row", 1)
    accumulated = accumulated.at[:, :window, :].add(lower_back)
    right_back = shifted(accumulated[:, :tile_rows, tile_cols:], "col", 1)
    accumulated = accumulated.at[:, :tile_rows, :window].add(right_back)
    object_gradient = accumulated[:, :tile_rows, :tile_cols]
    live_total = slots * lax.axis_size("row") * lax.axis_size("col") // 2
    summed = lax.psum(probe_total, ("row", "col"))
    probe_gradient = summed * (1.0 / math.sqrt(live_total))
    return (object_gradient, probe_gradient)


def solution(mesh):
    return jax.shard_map(
        per_device,
        mesh=mesh,
        in_specs=(
            P(None, "row", "col"),
            P(),
            P(("row", "col"), None, None),
            P(("row", "col"), None),
            P(),
        ),
        out_specs=(P(None, "row", "col"), P()),
        check_vma=False,
    )
```

profile of v0, /device:TPU:0, one launch (start us, length us, event | category | flops | bytes accessed | tf_op | source)
XLA Modules:
  0.0 586.3 jit_solution(8590055253525692689)
XLA Ops:
  14.0 23.9 %collective-permute-done = f32[2,512,256]{2,1,0:T(8,128)} collective-permute-done((f32[2,512,256]{2,1,0:T(8,128)}, f32[2,512,256]{2,1,0:T(8,128)}, u32[]{:S(2)}, u32[]{:S(2)}) %collective-permute-start) | collective-permute-done | bytes 1048608 | tf_op jit(solution)/shard_map/ppermute | solution.py:12
  42.4 3.9 copy.8
  52.7 3.8 pad_maximum_fusion
  56.5 69.6 %while.19 = (s32[]{:T(128)}, f32[2,768,768]{2,1,0:T(8,128)}, s32[16,3]{0,1:T(4,128)S(1)}, f32[16,2,256,384]{3,2,1,0:T(8,128)}, s32[]{:T(128)}) while((s32[]{:T(128)}, f32[2,768,768]{2,1,0:T(8,128)}, s32[16,3]{0,1:T(4,128)S(1)}, f32[16,2,256,384]{3,2,1,0:T(8,128)}, s32[]{:T(128)}) %tuple.85), condition=%wide.while_cond.2, body=%wide.while_body.2.sunk | while | flops 2 | bytes 1574505 | solution.py:73
  100.6 3.8 bitcast_dynamic-update-slice_fusion.2
  126.1 11.0 %fusion.8 = f32[16,2,256,256]{3,2,1,0:T(8,128)S(1)} fusion(f32[16,2,256,384]{3,2,1,0:T(8,128)} %get-tuple-element.145, s32[16,256]{1,0:T(8,128)S(1)} %iota_add_fusion.1), kind=kOutput, calls=%fused_computation.20 | convolution fusion | flops 9665249280 | bytes 20987904 | tf_op jit(solution)/shard_map/vmap(crk,kw->crw)/dot_general | solution.py:77
  137.2 3.8 subtract_convert_fusion
  141.7 10.2 %fusion.31 = f32[16,2,256,256]{2,3,0,1:T(8,128)} fusion(bf16[16,1,256,256]{3,2,1,0:T(8,128)(2,1)} %get-tuple-element.171, bf16[16,1,256,256]{3,2,1,0:T(8,128)(2,1)} %get-tuple-element.170, bf16[1,2,256,256]{2,3,0,1:T(8,128)(2,1)S(1)} %copy-done.8, bf16[1,2,256,256]{2,3,0,1:T(8,128)(2,1)S(1)} %copy-done.6, bf16[1,2,256,256]{2,3,1,0:T(8,128)(2,1)S(1)} %copy-done.7, ...), kind=kOutput, calls=%fused_computation.48 | convolution fusion | flops 4307550208 | bytes 13631488 | tf_op jit(solution)/shard_map/niab,iobd->noad/dot_general | solution.py:32
  151.8 6.6 %fusion.22 = f32[16,256,256]{1,2,0:T(8,128)} fusion(f32[16,2,256,256]{2,3,0,1:T(8,128)} %fusion.31, bf16[16,256,256]{1,2,0:T(8,128)(2,1)S(1)} %copy-done.1), kind=kLoop, calls=%fused_computation.33 | loop fusion | flops 7340032 | bytes 14680064 | tf_op jit(solution)/shard_map/sub | solution.py:43
  158.4 12.5 %fusion.28 = f32[16,2,256,256]{3,2,1,0:T(8,128)} fusion(bf16[1,2,256,256]{2,3,1,0:T(8,128)(2,1)S(1)} %copy-done.4, bf16[1,2,256,256]{2,3,1,0:T(8,128)(2,1)S(1)} %copy-done.5, f32[16,2,256,256]{2,3,0,1:T(8,128)} %fusion.31, f32[16,256,256]{1,2,0:T(8,128)} %fusion.22, bf16[1,2,256,256]{2,3,1,0:T(8,128)(2,1)} %get-tuple-element.189, ...), kind=kOutput, calls=%fused_computation.47 | convolution fusion | flops 4302569472 | bytes 22020096 | tf_op jit(solution)/shard_map/niab,iobd->noad/dot_general | solution.py:32
  170.9 7.1 %multiply_add_fusion = (f32[16,1,256,256]{3,2,1,0:T(8,128)S(1)}, f32[16,1,256,256]{3,2,1,0:T(8,128)S(1)}, f32[16,1,256,256]{3,2,1,0:T(8,128)S(1)}, f32[16,1,256,256]{3,2,1,0:T(8,128)S(1)}) fusion(f32[16,2,256,256]{3,2,1,0:T(8,128)} %fusion.28, f32[16,2,256,256]{3,2,1,0:T(8,128)} %copy-done, f32[256,256]{1,0:T(8,128)S(1)} %copy-done.2, ...), kind=kLoop, calls=%fused_computation.42 | loop fusion | flops 12582912 | bytes 34078720 | tf_op jit(solution)/shard_map/add | solution.py:55
  178.0 4.7 fusion.6
  185.2 219.0 %while.18 = (s32[]{:T(128)}, f32[2,768,768]{2,1,0:T(8,128)}, s32[16,2]{0,1:T(2,128)S(1)}, f32[16,2,256,256]{3,2,1,0:T(8,128)}, s32[]{:T(128)}, /*index=5*/s32[]{...) while((s32[]{:T(128)}, f32[2,768,768]{2,1,0:T(8,128)}, s32[16,2]{0,1:T(2,128)S(1)}, ...), condition=%wide.region_1.2_spmd, body=%wide.region_0.1_spmd.sunk | while | flops 604274944 | bytes 3672963 | solution.py:128
  193.1 5.9 %dynamic_update_slice.11 = f32[2,768,768]{2,1,0:T(8,128)} dynamic-update-slice(f32[2,768,768]{2,1,0:T(8,128)} %get-tuple-element.283, f32[2,256,384]{2,1,0:T(8,128)S(1)} %convolution_add_fusion.2, s32[]{:T(128)} %constant.187.clone.1..sunk, s32[]{:T(128)S(6)} %select_n.162, s32[]{:T(128)S(6)} %select_n.164) | dynamic-update-slice | bytes 1572868 | tf_op jit(solution)/shard_map/while/body/eval_jaxpr/dynamic_update_slice | solution.py:89
  206.9 5.8 dynamic_update_slice.11
  220.6 5.9 %dynamic_update_slice.11 = f32[2,768,768]{2,1,0:T(8,128)} dynamic-update-slice(f32[2,768,768]{2,1,0:T(8,128)} %get-tuple-element.283, f32[2,256,384]{2,1,0:T(8,128)S(1)} %convolution_add_fusion.2, s32[]{:T(128)} %constant.187.clone.1..sunk, s32[]{:T(128)S(6)} %select_n.162, s32[]{:T(128)S(6)} %select_n.164) | dynamic-update-slice | bytes 1572868 | tf_op jit(solution)/shard_map/while/body/eval_jaxpr/dynamic_update_slice | solution.py:89
  234.4 5.8 dynamic_update_slice.11
  248.1 5.8 dynamic_update_slice.11
  261.7 5.3 dynamic_update_slice.11
  274.9 5.8 dynamic_update_slice.11
  288.6 5.8 dynamic_update_slice.11
  302.2 5.8 dynamic_update_slice.11
  316.0 5.9 %dynamic_update_slice.11 = f32[2,768,768]{2,1,0:T(8,128)} dynamic-update-slice(f32[2,768,768]{2,1,0:T(8,128)} %get-tuple-element.283, f32[2,256,384]{2,1,0:T(8,128)S(1)} %convolution_add_fusion.2, s32[]{:T(128)} %constant.187.clone.1..sunk, s32[]{:T(128)S(6)} %select_n.162, s32[]{:T(128)S(6)} %select_n.164) | dynamic-update-slice | bytes 1572868 | tf_op jit(solution)/shard_map/while/body/eval_jaxpr/dynamic_update_slice | solution.py:89
  329.7 5.9 dynamic_update_slice.11
  343.4 6.0 %dynamic_update_slice.11 = f32[2,768,768]{2,1,0:T(8,128)} dynamic-update-slice(f32[2,768,768]{2,1,0:T(8,128)} %get-tuple-element.283, f32[2,256,384]{2,1,0:T(8,128)S(1)} %convolution_add_fusion.2, s32[]{:T(128)} %constant.187.clone.1..sunk, s32[]{:T(128)S(6)} %select_n.162, s32[]{:T(128)S(6)} %select_n.164) | dynamic-update-slice | bytes 1572868 | tf_op jit(solution)/shard_map/while/body/eval_jaxpr/dynamic_update_slice | solution.py:89
  357.3 5.8 dynamic_update_slice.11
  370.9 5.8 dynamic_update_slice.11
  384.6 6.0 %dynamic_update_slice.11 = f32[2,768,768]{2,1,0:T(8,128)} dynamic-update-slice(f32[2,768,768]{2,1,0:T(8,128)} %get-tuple-element.283, f32[2,256,384]{2,1,0:T(8,128)S(1)} %convolution_add_fusion.2, s32[]{:T(128)} %constant.187.clone.1..sunk, s32[]{:T(128)S(6)} %select_n.162, s32[]{:T(128)S(6)} %select_n.164) | dynamic-update-slice | bytes 1572868 | tf_op jit(solution)/shard_map/while/body/eval_jaxpr/dynamic_update_slice | solution.py:89
  398.4 5.8 dynamic_update_slice.11
  405.7 8.9 %collective-permute-start.2 = (f32[2,256,768]{2,1,0:T(8,128)S(1)}, f32[2,256,768]{2,1,0:T(8,128)S(1)}, u32[]{:S(2)}, u32[]{:S(2)}) collective-permute-start(f32[2,256,768]{2,1,0:T(8,128)S(1)} %slice.122), channel_id=1, source_target_pairs={{0,4},{4,8},{8,12},{12,16},{16,20},{20,24},{24,28},{1,5},{5,9},{9,... | collective-permute-start | bytes 4718600 | tf_op jit(solution)/shard_map/ppermute | solution.py:12
  421.6 3.9 collective-permute-start.3
  426.2 145.2 %all-reduce.2.cloned.1.call-done = f32[2,256,256]{2,1,0:T(8,128)} async-done(((f32[2,256,256]{2,1,0:T(8,128)}), f32[2,256,256]{2,1,0:T(8,128)}) %all-reduce.2.cloned.1.call-update) | async-done | bytes 524304 | tf_op jit(solution)/shard_map/psum | solution.py:135
  (149 shorter events, 145.1 us)
Async XLA Ops:
  7.2 6.8 %copy-start.9 = (s32[16,2]{0,1:T(2,128)S(1)}, s32[16,2]{0,1:T(2,128)}, u32[]{:S(2)}) copy-start(s32[16,2]{0,1:T(2,128)} %param.14) | copy-start | bytes 388
  7.2 564.3 %all-reduce.2.cloned.1.call-start = ((), (), s32[]{:S(2)}) async-start(), calls=%async_computation | async-start | bytes 1048576 | tf_op jit(solution)/shard_map/psum | solution.py:135
  9.5 28.4 %collective-permute-start = (f32[2,512,256]{2,1,0:T(8,128)}, f32[2,512,256]{2,1,0:T(8,128)}, u32[]{:S(2)}, u32[]{:S(2)}) collective-permute-start(f32[2,512,256]{2,1,0:T(8,128)} %slice.110), channel_id=1, source_target_pairs={{1,0},{2,1},{3,2},{5,4},{6,5},{7,6},{9,8},{10,9},{11,10},{13,12},{... | collective-permute-start | bytes 3145736 | tf_op jit(solution)/shard_map/ppermute | solution.py:12
  40.4 12.3 %collective-permute-start.1 = (f32[2,256,768]{2,1,0:T(8,128)}, f32[2,256,768]{2,1,0:T(8,128)}, u32[]{:S(2)}, u32[]{:S(2)}) collective-permute-start(f32[2,256,768]{2,1,0:T(8,128)} %slice.141), channel_id=1, source_target_pairs={{4,0},{8,4},{12,8},{16,12},{20,16},{24,20},{28,24},{5,1},{9,5},{13... | collective-permute-start | bytes 4718600 | tf_op jit(solution)/shard_map/ppermute | solution.py:12
  126.1 11.1 %copy-start.2 = (f32[256,256]{1,0:T(8,128)S(1)}, f32[256,256]{1,0:T(8,128)}, u32[]{:S(2)}) copy-start(f32[256,256]{1,0:T(8,128)} %get-tuple-element.175) | copy-start | bytes 786436
  137.1 4.5 copy-start
  137.1 4.5 copy-start.6
  137.1 4.5 copy-start.7
  137.2 4.5 copy-start.8
  141.7 10.2 %copy-start.1 = (bf16[16,256,256]{1,2,0:T(8,128)(2,1)S(1)}, bf16[16,256,256]{1,2,0:T(8,128)(2,1)}, u32[]{:S(2)}) copy-start(bf16[16,256,256]{1,2,0:T(8,128)(2,1)} %copy.8) | copy-start | bytes 6291460
  151.8 6.6 %copy-start.3 = (bf16[1,2,256,256]{2,3,1,0:T(8,128)(2,1)S(1)}, bf16[1,2,256,256]{2,3,1,0:T(8,128)(2,1)}, u32[]{:S(2)}) copy-start(bf16[1,2,256,256]{2,3,1,0:T(8,128)(2,1)} %get-tuple-element.176) | copy-start | bytes 786436
  151.8 6.6 %copy-start.4 = (bf16[1,2,256,256]{2,3,1,0:T(8,128)(2,1)S(1)}, bf16[1,2,256,256]{2,3,1,0:T(8,128)(2,1)}, u32[]{:S(2)}) copy-start(bf16[1,2,256,256]{2,3,1,0:T(8,128)(2,1)} %get-tuple-element.177) | copy-start | bytes 786436
  151.8 6.6 %copy-start.5 = (bf16[1,2,256,256]{2,3,1,0:T(8,128)(2,1)S(1)}, bf16[1,2,256,256]{2,3,1,0:T(8,128)(2,1)}, u32[]{:S(2)}) copy-start(bf16[1,2,256,256]{2,3,1,0:T(8,128)(2,1)} %get-tuple-element.188) | copy-start | bytes 786436
  405.7 11.8 %collective-permute-start.2 = (f32[2,256,768]{2,1,0:T(8,128)S(1)}, f32[2,256,768]{2,1,0:T(8,128)S(1)}, u32[]{:S(2)}, u32[]{:S(2)}) collective-permute-start(f32[2,256,768]{2,1,0:T(8,128)S(1)} %slice.122), channel_id=1, source_target_pairs={{0,4},{4,8},{8,12},{12,16},{16,20},{20,24},{24,28},{1,5},{5,9},{9,... | collective-permute-start | bytes 4718600 | tf_op jit(solution)/shard_map/ppermute | solution.py:12
  421.6 151.7 %collective-permute-start.3 = (f32[2,512,256]{2,1,0:T(8,128)S(1)}, f32[2,512,256]{2,1,0:T(8,128)S(1)}, u32[]{:S(2)}, u32[]{:S(2)}) collective-permute-start(f32[2,512,256]{2,1,0:T(8,128)S(1)} %slice.149), channel_id=1, source_target_pairs={{0,1},{1,2},{2,3},{4,5},{5,6},{6,7},{8,9},{9,10},{10,11},{12,13},{... | collective-permute-start | bytes 3145736 | tf_op jit(solution)/shard_map/ppermute | solution.py:12
Sparse Core Ops, SparseCore 0:
  425.7 145.7 all-reduce.1
where the time goes:
time: 592 us; the launch traced here: 586 us
  local copies, waits for them, and re-layouts  196 us (33%)
  waiting for transfers between devices  172 us (29%)
  loops' own time  84.8 us (14%)
  matrix products  64.5 us (11%)
  other arithmetic  39.9 us (7%)
  starting transfers between devices  15.3 us (3%)
  between operations  14.2 us (2%)
    psum x1, waiting for transfers between devices, per_device(): summed = lax.psum(probe_total, ('row', 'col'))  145 us
    dynamic_update_slice x16, local copies, waits for them, and re-layouts, add_patch(): lax.dynamic_update_slice(current, block + spread, (zero_index, corner_row...  92.9 us
    another operation x1, loops' own time, per_device(): accumulated = lax.fori_loop(0, slots, add_slot, accumulated)  84.8 us
    gather x48, local copies, waits for them, and re-layouts  69.6 us
    dot_general x16, matrix products, add_patch(): jnp.einsum('crw,kw->crk', terms, table, precision=lax.Precision.HIGHEST)  30.8 us
    ppermute x4, waiting for transfers between devices, shifted(): lax.ppermute(value, axis, [(source, source + steps) for source in range(l...  26.8 us
    dot_general x2, matrix products, transform(): jnp.einsum('niab,iobd->noad', half, right, preferred_element_type=jnp.flo...  22.6 us
    ppermute x4, starting transfers between devices, shifted(): lax.ppermute(value, axis, [(source, source + steps) for source in range(l...  15.3 us
  transfers between devices with their start and end apart: 5, of which 3 were waited for; matrix products, arithmetic and copies ran while one was open for 3% of the time, Pallas kernels for 0%

commit v1 on v0

v1 whole, which is shorter than its diff:
```python
import functools
import math

import jax
import jax.numpy as jnp
import numpy as np
from jax import lax
from jax.experimental import pallas as pl
from jax.experimental.pallas import tpu as pltpu
from jax.sharding import PartitionSpec as P

LANE = 128
CHUNK = 32
F32 = jnp.float32
BF16 = jnp.bfloat16


def shifted(value, axis, steps):
    count = lax.axis_size(axis)
    leading, last = (max(0, -steps), min(count, count - steps))
    return lax.ppermute(value, axis, [(source, source + steps) for source in range(leading, last)])


def dft_blocks(window):
    index = np.arange(window)
    angle = (index[:, None] * index[None, :] % window) * (2.0 * math.pi / window)
    cosine = np.cos(angle) / math.sqrt(window)
    sine = np.sin(angle) / math.sqrt(window)
    forward = np.block([[cosine, sine], [-sine, cosine]])
    inverse = np.block([[cosine, -sine], [sine, cosine]])
    return forward.astype(BF16), inverse.astype(BF16)


def slot_steps(window, tiles_count, class_low, class_high, tile_cols, columns, refs):
    (offs, counts, amplitude, forward, inverse, probe, ext, acc, pacc) = refs["io"]
    (chosen, amp, patch, ext_wave, half, resid, back_half, amp_sem) = refs["scratch"]
    slots = offs.shape[0]
    live = counts[lax.axis_index("row") * columns + lax.axis_index("col")]
    tile_rows = refs["tile_rows"]

    def first_tile(col):
        return lax.div(jnp.maximum(col - 1, 0), LANE)

    def pick(j, n):
        tile = first_tile(lax.rem(offs[j, 1], tile_cols))
        chosen[n] = j
        take = (j < live) & (tile >= class_low) & (tile < class_high)
        return n + take.astype(jnp.int32)

    total = lax.fori_loop(0, slots, pick, jnp.int32(0))

    def fetch(i):
        buffer = lax.rem(i, 2)
        return pltpu.make_async_copy(amplitude.at[chosen[i]], amp.at[buffer], amp_sem.at[buffer])

    @pl.when(total > 0)
    def _():
        fetch(0).start()

    refs["ready"]()
    lane = lax.broadcasted_iota(jnp.int32, (CHUNK, LANE), 1)

    def body(i, carry):
        @pl.when(i + 1 < total)
        def _():
            fetch(i + 1).start()

        j = chosen[i]
        row = lax.rem(offs[j, 0], tile_rows)
        col = lax.rem(offs[j, 1], tile_cols)
        tile = first_tile(col)
        rest = col - tile * LANE
        tile = tile - class_low
        turn = lax.rem(LANE - rest, LANE)
        head = lane < LANE - rest
        for base in range(0, window, CHUNK):
            rows = pl.ds(row + base, CHUNK)
            here = slice(base, base + CHUNK)
            planes = []
            for plane in range(2):
                turned = [
                    pltpu.roll(ext[plane, tile + k, rows, :], turn, 1) for k in range(3)
                ]
                planes.append(
                    [jnp.where(head, turned[k], turned[k + 1]) for k in range(2)]
                )
            for k in range(2):
                cols = slice(k * LANE, (k + 1) * LANE)
                real, imag = planes[0][k], planes[1][k]
                patch[0, here, cols] = real
                patch[1, here, cols] = imag
                probe_real, probe_imag = probe[0, here, cols], probe[1, here, cols]
                ext_wave[base : base + CHUNK, cols] = (
                    probe_real * real - probe_imag * imag
                ).astype(BF16)
                ext_wave[window + base : window + base + CHUNK, cols] = (
                    probe_real * imag + probe_imag * real
                ).astype(BF16)
        mid = jnp.dot(forward[...], ext_wave[...], preferred_element_type=F32).astype(BF16)
        half[:, :window] = mid[:window]
        half[:, window:] = mid[window:]
        far = jnp.dot(half[...], inverse[...], preferred_element_type=F32)
        fetch(i).wait()
        buffer = lax.rem(i, 2)
        for base in range(0, window, CHUNK):
            here = slice(base, base + CHUNK)
            real, imag = far[here, :window], far[here, window:]
            level = amp[buffer, here, :].astype(F32)
            factor = 1.0 - level * lax.rsqrt(real * real + imag * imag + 0.25)
            resid[here, :] = (real * factor).astype(BF16)
            resid[window + base : window + base + CHUNK, :] = (imag * factor).astype(BF16)
        mid = jnp.dot(inverse[...], resid[...], preferred_element_type=F32).astype(BF16)
        back_half[:, :window] = mid[:window]
        back_half[:, window:] = mid[window:]
        back = jnp.dot(back_half[...], forward[...], preferred_element_type=F32)
        tail = lane >= rest
        for base in range(0, window, CHUNK):
            rows = pl.ds(row + base, CHUNK)
            here = slice(base, base + CHUNK)
            terms = [[], []]
            for k in range(2):
                cols = slice(k * LANE, (k + 1) * LANE)
                real = back[here, k * LANE : (k + 1) * LANE]
                imag = back[here, window + k * LANE : window + (k + 1) * LANE]
                probe_real, probe_imag = probe[0, here, cols], probe[1, here, cols]
                patch_real, patch_imag = patch[0, here, cols], patch[1, here, cols]
                pacc[0, here, cols] += patch_real * real + patch_imag * imag
                pacc[1, here, cols] += patch_real * imag - patch_imag * real
                terms[0].append(pltpu.roll(probe_real * real + probe_imag * imag, lax.rem(rest, LANE), 1))
                terms[1].append(pltpu.roll(probe_real * imag - probe_imag * real, lax.rem(rest, LANE), 1))
            for plane in range(2):
                first, second = terms[plane]
                acc[plane, tile, rows, :] += jnp.where(tail, first, 0.0)
                acc[plane, tile + 1, rows, :] += jnp.where(tail, second, first)
                acc[plane, tile + 2, rows, :] += jnp.where(tail, 0.0, second)
        return carry

    lax.fori_loop(0, total, body, 0)


def run_copies(copies):
    for copy in copies:
        copy.start()
    return copies


def make_scratch(window, tiles, rows, copies):
    return [
        pltpu.VMEM((2, tiles, rows, LANE), F32),
        pltpu.VMEM((2, tiles, rows, LANE), F32),
        pltpu.VMEM((2, window, window), F32),
        pltpu.SMEM((32,), jnp.int32),
        pltpu.VMEM((2, window, window), BF16),
        pltpu.VMEM((2, window, window), F32),
        pltpu.VMEM((2 * window, window), BF16),
        pltpu.VMEM((window, 2 * window), BF16),
        pltpu.VMEM((2 * window, window), BF16),
        pltpu.VMEM((window, 2 * window), BF16),
        pltpu.SemaphoreType.DMA((2,)),
        pltpu.SemaphoreType.DMA((copies,)),
    ]


SMEM = pl.BlockSpec(memory_space=pltpu.SMEM)
VMEM = pl.BlockSpec(memory_space=pltpu.VMEM)
HBM = pl.BlockSpec(memory_space=pl.ANY)


def span(tile, count=1):
    return pl.ds(tile * LANE, count * LANE)


def inner_kernel(
    shape, offs, counts, amplitude, forward, inverse, probe, tile_in, lower_in,
    own, strip, spill, probe_sum,
    ext, acc, pacc, chosen, amp, patch, ext_wave, half, resid, back_half, amp_sem, sems,
):
    rows, cols, window, columns = shape
    tiles = cols // LANE
    copies = []
    for k in range(tiles):
        copies.append(pltpu.make_async_copy(
            tile_in.at[:, :, span(k)], ext.at[:, k, pl.ds(0, rows), :], sems.at[2 * k]))
        copies.append(pltpu.make_async_copy(
            lower_in.at[:, :, span(k)], ext.at[:, k, pl.ds(rows, window), :], sems.at[2 * k + 1]))
    run_copies(copies)
    acc[...] = jnp.zeros_like(acc)
    pacc[...] = jnp.zeros_like(pacc)

    def ready():
        for copy in copies:
            copy.wait()

    slot_steps(window, tiles, 0, tiles - 2, cols, columns, dict(
        io=(offs, counts, amplitude, forward, inverse, probe, ext, acc, pacc),
        scratch=(chosen, amp, patch, ext_wave, half, resid, back_half, amp_sem),
        tile_rows=rows, ready=ready))
    out = []
    for k in range(tiles - 2):
        out.append(pltpu.make_async_copy(
            acc.at[:, k, pl.ds(0, rows), :], own.at[:, :, span(k)], sems.at[2 * k]))
        out.append(pltpu.make_async_copy(
            acc.at[:, k, pl.ds(rows, window), :], strip.at[:, :, span(k)], sems.at[2 * k + 1]))
    out.append(pltpu.make_async_copy(acc.at[:, pl.ds(tiles - 2, 2)], spill, sems.at[2 * tiles]))
    out.append(pltpu.make_async_copy(pacc, probe_sum, sems.at[2 * tiles + 1]))
    run_copies(out)
    for copy in out:
        copy.wait()


def near_kernel(
    shape, offs, counts, amplitude, forward, inverse, probe, tile_in, lower_in, right_in, corner_in,
    spill_in, probe_in, own_in, strip_in,
    own, strip, spill, probe_sum,
    ext, acc, pacc, chosen, amp, patch, ext_wave, half, resid, back_half, amp_sem, sems,
):
    rows, cols, window, columns = shape
    last = cols // LANE
    copies = [
        pltpu.make_async_copy(spill_in, acc.at[:, pl.ds(0, 2)], sems.at[0]),
        pltpu.make_async_copy(probe_in, pacc, sems.at[1]),
        pltpu.make_async_copy(right_in, ext.at[:, 2, pl.ds(0, rows), :], sems.at[2]),
        pltpu.make_async_copy(corner_in, ext.at[:, 2, pl.ds(rows, window), :], sems.at[3]),
    ]
    for k in range(2):
        copies.append(pltpu.make_async_copy(
            tile_in.at[:, :, span(last - 2 + k)], ext.at[:, k, pl.ds(0, rows), :], sems.at[4 + 2 * k]))
        copies.append(pltpu.make_async_copy(
            lower_in.at[:, :, span(last - 2 + k)], ext.at[:, k, pl.ds(rows, window), :], sems.at[5 + 2 * k]))
    run_copies(copies)
    acc[:, 2] = jnp.zeros_like(acc[:, 2])

    def ready():
        for copy in copies:
            copy.wait()

    slot_steps(window, 3, last - 2, last - 1, cols, columns, dict(
        io=(offs, counts, amplitude, forward, inverse, probe, ext, acc, pacc),
        scratch=(chosen, amp, patch, ext_wave, half, resid, back_half, amp_sem),
        tile_rows=rows, ready=ready))
    out = [
        pltpu.make_async_copy(acc.at[:, 0, pl.ds(0, rows), :], own.at[:, :, span(last - 2)], sems.at[0]),
        pltpu.make_async_copy(acc.at[:, 0, pl.ds(rows, window), :], strip.at[:, :, span(last - 2)], sems.at[1]),
        pltpu.make_async_copy(acc.at[:, pl.ds(1, 2)], spill, sems.at[2]),
        pltpu.make_async_copy(pacc, probe_sum, sems.at[3]),
    ]
    run_copies(out)
    for copy in out:
        copy.wait()


def far_kernel(
    shape, offs, counts, amplitude, forward, inverse, probe, tile_in, lower_in, right_in, corner_in,
    far_top, far_bottom, far_corner, spill_in, probe_in, own_in, strip_in,
    own, strip, top, bottom, corner, probe_sum,
    ext, acc, pacc, chosen, amp, patch, ext_wave, half, resid, back_half, amp_sem, sems,
):
    rows, cols, window, columns = shape
    last = cols // LANE - 1
    copies = [
        pltpu.make_async_copy(spill_in, acc.at[:, pl.ds(0, 2)], sems.at[0]),
        pltpu.make_async_copy(probe_in, pacc, sems.at[1]),
        pltpu.make_async_copy(right_in, ext.at[:, 1, pl.ds(0, rows), :], sems.at[2]),
        pltpu.make_async_copy(corner_in, ext.at[:, 1, pl.ds(rows, window), :], sems.at[3]),
        pltpu.make_async_copy(tile_in.at[:, :, span(last)], ext.at[:, 0, pl.ds(0, rows), :], sems.at[4]),
        pltpu.make_async_copy(lower_in.at[:, :, span(last)], ext.at[:, 0, pl.ds(rows, window), :], sems.at[5]),
        pltpu.make_async_copy(far_top, ext.at[:, 2, pl.ds(0, window), :], sems.at[6]),
        pltpu.make_async_copy(far_bottom, ext.at[:, 2, pl.ds(window, rows - window), :], sems.at[7]),
        pltpu.make_async_copy(far_corner, ext.at[:, 2, pl.ds(rows, window), :], sems.at[8]),
    ]
    run_copies(copies)
    acc[:, 2] = jnp.zeros_like(acc[:, 2])

    def ready():
        for copy in copies:
            copy.wait()

    slot_steps(window, 3, last, last + 1, cols, columns, dict(
        io=(offs, counts, amplitude, forward, inverse, probe, ext, acc, pacc),
        scratch=(chosen, amp, patch, ext_wave, half, resid, back_half, amp_sem),
        tile_rows=rows, ready=ready))
    out = [
        pltpu.make_async_copy(acc.at[:, 0, pl.ds(0, rows), :], own.at[:, :, span(last)], sems.at[0]),
        pltpu.make_async_copy(acc.at[:, 0, pl.ds(rows, window), :], strip.at[:, :, span(last)], sems.at[1]),
        pltpu.make_async_copy(pacc, probe_sum, sems.at[2]),
    ]
    for k in range(2):
        out.append(pltpu.make_async_copy(
            acc.at[:, 1 + k, pl.ds(0, window), :], top.at[:, :, span(k)], sems.at[3 + 3 * k]))
        out.append(pltpu.make_async_copy(
            acc.at[:, 1 + k, pl.ds(window, rows - window), :], bottom.at[:, :, span(k)], sems.at[4 + 3 * k]))
        out.append(pltpu.make_async_copy(
            acc.at[:, 1 + k, pl.ds(rows, window), :], corner.at[:, :, span(k)], sems.at[5 + 3 * k]))
    run_copies(out)
    for copy in out:
        copy.wait()


def exchange_sum(value, window):
    for axis in ("row", "col"):
        count = lax.axis_size(axis)
        step = 1
        while step < count:
            value = value + lax.ppermute(value, axis, [(k, k ^ step) for k in range(count)])
            step *= 2
    return value


def per_device(object_field, illumination, amplitude, offsets, slot_counts):
    rows, cols = object_field.shape[1:]
    window = illumination.shape[1]
    slots = offsets.shape[0]
    columns = lax.axis_size("col")
    shape = (rows, cols, window, columns)
    forward, inverse = dft_blocks(window)
    forward, inverse = jnp.asarray(forward), jnp.asarray(inverse)

    near = shifted(object_field[:, :, :LANE], "col", -1)
    lower = shifted(object_field[:, :window, :], "row", -1)
    far_top = shifted(object_field[:, :window, LANE:window], "col", -1)
    far_bottom = shifted(object_field[:, window:, LANE:window], "col", -1)
    near_corner = shifted(near[:, :window], "row", -1)
    far_corner = shifted(far_top, "row", -1)

    def sds(*dims):
        return jax.ShapeDtypeStruct(dims, F32)

    common = (offsets, slot_counts, amplitude, forward, inverse, illumination)
    common_specs = [SMEM, SMEM, HBM, VMEM, VMEM, VMEM]
    reach = rows + window
    params = pltpu.CompilerParams(vmem_limit_bytes=48 * 1024 * 1024)
    flops = 16 * 2 * window**3

    def cost(count):
        return pl.CostEstimate(flops=flops * count, bytes_accessed=8 * 2**20, transcendentals=0)

    own, strip, spill, probe_sum = pl.pallas_call(
        functools.partial(inner_kernel, shape),
        out_shape=[sds(2, rows, cols), sds(2, window, cols), sds(2, 2, reach, LANE), sds(2, window, window)],
        in_specs=common_specs + [HBM] * 2,
        out_specs=[HBM] * 4,
        scratch_shapes=make_scratch(window, cols // LANE, reach, 12),
        compiler_params=params,
        cost_estimate=cost(8),
        name="inner_slots",
    )(*common, object_field, lower)
    own, strip, spill, probe_sum = pl.pallas_call(
        functools.partial(near_kernel, shape),
        out_shape=[sds(2, rows, cols), sds(2, window, cols), sds(2, 2, reach, LANE), sds(2, window, window)],
        in_specs=common_specs + [HBM] * 8,
        out_specs=[HBM] * 4,
        input_output_aliases={12: 0, 13: 1},
        scratch_shapes=make_scratch(window, 3, reach, 12),
        compiler_params=params,
        cost_estimate=cost(4),
        name="near_slots",
    )(*common, object_field, lower, near, near_corner, spill, probe_sum, own, strip)
    own, strip, top, bottom, corner, probe_sum = pl.pallas_call(
        functools.partial(far_kernel, shape),
        out_shape=[sds(2, rows, cols), sds(2, window, cols), sds(2, window, window),
                   sds(2, rows - window, window), sds(2, window, window), sds(2, window, window)],
        in_specs=common_specs + [HBM] * 11,
        out_specs=[HBM] * 6,
        input_output_aliases={15: 0, 16: 1},
        scratch_shapes=make_scratch(window, 3, reach, 12),
        compiler_params=params,
        cost_estimate=cost(4),
        name="far_slots",
    )(*common, object_field, lower, near, near_corner, far_top, far_bottom, far_corner,
      spill, probe_sum, own, strip)

    bottom_back = shifted(bottom, "col", 1)
    corner_back = shifted(corner, "row", 1)
    strip_back = shifted(strip, "row", 1)
    top_back = shifted(top + corner_back, "col", 1)
    own = own.at[:, :window, :].add(strip_back)
    own = own.at[:, window:, :window].add(bottom_back)
    own = own.at[:, :window, :window].add(top_back)
    summed = exchange_sum(probe_sum, window)
    live_total = slots * lax.axis_size("row") * lax.axis_size("col") // 2
    return own, summed * (1.0 / math.sqrt(live_total))


def solution(mesh):
    return jax.shard_map(
        per_device,
        mesh=mesh,
        in_specs=(
            P(None, "row", "col"),
            P(),
            P(("row", "col"), None, None),
            P(("row", "col"), None),
            P(),
        ),
        out_specs=(P(None, "row", "col"), P()),
        check_vma=False,
    )
```

time: 592 us -> 170 us (0.29)
  local copies, waits for them, and re-layouts: 196 us -> 8.39 us
  loops' own time: 84.8 us -> 0 us
  waiting for transfers between devices: 172 us -> 87.8 us
  matrix products: 64.5 us -> 0 us
  other arithmetic: 39.9 us -> 1.8 us
  Pallas kernels: 0 us -> 37.6 us
  starting transfers between devices: 15.3 us -> 32.3 us
  between operations: 14.2 us -> 0.96 us
    psum x1 -> x0, waiting for transfers between devices: 145 us -> none  [per_device(): summed = lax.psum(probe_total, ('row', 'col'))]
    dynamic_update_slice x16 -> x0, local copies, waits for them, and re-layouts: 92.9 us -> none  [add_patch(): lax.dynamic_update_slice(current, block + spread, (zero_index, corner_row...]
    another operation x2 -> x0, loops' own time: 84.8 us -> none  [the longest x1 84.8 us: per_device(): accumulated = lax.fori_loop(0, slots, add_slot, accumulated)]
    gather x48 -> x0, local copies, waits for them, and re-layouts: 69.6 us -> none
    dot_general x19 -> x0, matrix products: 64.5 us -> none  [the longest x16 30.8 us: add_patch(): jnp.einsum('crw,kw->crk', terms, table, precision=lax.Precision.HIGHEST)]
    ppermute x0 -> x5, waiting for transfers between devices: none -> 48.3 us  [exchange_sum(): lax.ppermute(value, axis, [(k, k ^ step) for k in range(count)])]
    pallas_call x0 -> x3, Pallas kernels: none -> 37.6 us  [the longest x1 20.6 us: per_device(): pl.pallas_call(functools.partial(inner_kernel, shape), out_shape=[sds(2,...]
    ppermute x0 -> x5, starting transfers between devices: none -> 17.2 us  [exchange_sum(): lax.ppermute(value, axis, [(k, k ^ step) for k in range(count)])]
  transfers between devices with their start and end apart: 5 -> 15, of which waited for: 3 -> 8; matrix products, arithmetic and copies ran while one was open for 3% -> 3% of each run, Pallas kernels for 0% -> 18%
where the time goes in v1:
time: 170 us; the launch traced here: 169 us
  waiting for transfers between devices  87.8 us (52%)
  Pallas kernels  37.6 us (22%)
  starting transfers between devices  32.3 us (19%)
  local copies, waits for them, and re-layouts  8.39 us (5%)
  other arithmetic  1.8 us (1%)
    ppermute x5, waiting for transfers between devices, exchange_sum(): lax.ppermute(value, axis, [(k, k ^ step) for k in range(count)])  48.3 us
    ppermute x10, waiting for transfers between devices, shifted(): lax.ppermute(value, axis, [(source, source + steps) for source in range(l...  39.5 us
    pallas_call x1, Pallas kernels, per_device(): pl.pallas_call(functools.partial(inner_kernel, shape), out_shape=[sds(2,...  20.6 us
    ppermute x5, starting transfers between devices, exchange_sum(): lax.ppermute(value, axis, [(k, k ^ step) for k in range(count)])  17.2 us
    ppermute x10, starting transfers between devices, shifted(): lax.ppermute(value, axis, [(source, source + steps) for source in range(l...  15.1 us
    pallas_call x1, Pallas kernels, per_device(): pl.pallas_call(functools.partial(near_kernel, shape), out_shape=[sds(2, r...  9.68 us
    pallas_call x1, Pallas kernels, per_device(): pl.pallas_call(functools.partial(far_kernel, shape), out_shape=[sds(2, ro...  7.27 us
  transfers between devices with their start and end apart: 15, of which 8 were waited for; matrix products, arithmetic and copies ran while one was open for 3% of the time, Pallas kernels for 18%

profile of v1, /device:TPU:0, one launch (start us, length us, event | category | flops | bytes accessed | tf_op | source)
XLA Modules:
  0.0 168.8 jit_solution(4707732443597217821)
XLA Ops:
  0.7 2.4 %slice.97 = f32[2,256,512]{2,1,0:T(8,128)} slice(f32[2,512,512]{2,1,0:T(8,128)} %tile_in.5), slice={[0:2], [0:256], [0:512]} | slice | bytes 2097152 | tf_op jit(solution)/shard_map/slice | solution.py:319
  3.1 1.3 collective-permute-start
  4.3 1.9 %slice.98 = f32[2,512,128]{2,1,0:T(8,128)} slice(f32[2,512,512]{2,1,0:T(8,128)} %tile_in.5), slice={[0:2], [0:512], [0:128]} | slice | bytes 1048576 | tf_op jit(solution)/shard_map/slice | solution.py:318
  6.2 1.3 collective-permute-start.1
  7.5 1.9 %fusion.2 = (f32[2,256,128]{2,1,0:T(8,128)}, f32[2,256,128]{2,1,0:T(8,128)}) fusion(f32[2,512,512]{2,1,0:T(8,128)} %tile_in.5), kind=kLoop, calls=%fused_computation.6 | loop fusion | bytes 1048576 | tf_op jit(solution)/shard_map/slice | solution.py:321
  9.4 1.3 collective-permute-start.3
  10.7 1.3 collective-permute-start.4
  12.1 17.3 %collective-permute-done.3.far_top = f32[2,256,128]{2,1,0:T(8,128)S(1)} collective-permute-done((f32[2,256,128]{2,1,0:T(8,128)}, f32[2,256,128]{2,1,0:T(8,128)S(1)}, u32[]{:S(2)}, u32[]{:S(2)}) %collective-permute-start.3) | collective-permute-done | bytes 262176 | tf_op jit(solution)/shard_map/ppermute | solution.py:21
  29.4 1.3 collective-permute-start.5
  30.7 1.3 collective-permute-start.2
  32.1 20.6 %inner_slots.1 = (f32[2,512,512]{2,1,0:T(8,128)}, f32[2,256,512]{2,1,0:T(8,128)S(1)}, f32[2,2,768,128]{3,2,1,0:T(8,128)S(1)}, f32[2,256,256]{2,1,0:T(8,128)S(1)}) custom-call(s32[16,2]{1,0:T(8,128)S(1)} %copy.15.offs, s32[32]{0:T(128)S(1)} %copy-done.6, bf16[16,256,256]{2,1,0:T(8,128)(2,1)} %amplitude.5, bf16[512,512]{1,0:T(8,128)(2,1)S(1)} %copy-done.4, ...), custom_call_target="tpu_custom_call" | custom-call | flops 4294967296 | bytes 8388608 | tf_op jit(solution)/shard_map/inner_slots/pallas_call | solution.py:337
  52.7 1.1 copy-done.5
  53.9 9.7 %near_slots.1 = (f32[2,512,512]{2,1,0:T(8,128)}, f32[2,256,512]{2,1,0:T(8,128)S(1)}, f32[2,2,768,128]{3,2,1,0:T(8,128)}, f32[2,256,256]{2,1,0:T(8,128)S(1)}) custom-call(s32[16,2]{1,0:T(8,128)S(1)} %copy.15.offs, s32[32]{0:T(128)S(1)} %copy-done.6, bf16[16,256,256]{2,1,0:T(8,128)(2,1)} %amplitude.5, ...), custom_call_target="tpu_custom_call", output_to_operand_aliasing={{0}: (12, {}), {1}: (13, {})} | custom-call | flops 2147483648 | bytes 8388608 | tf_op jit(solution)/shard_map/near_slots/pallas_call | solution.py:347
  63.6 1.0 copy-done.1
  64.5 7.3 %far_slots.1 = (f32[2,512,512]{2,1,0:T(8,128)}, f32[2,256,512]{2,1,0:T(8,128)}, f32[2,256,256]{2,1,0:T(8,128)S(1)}, f32[2,256,256]{2,1,0:T(8,128)S(1)}, f32[2,25...) custom-call(s32[16,2]{1,0:T(8,128)S(1)} %copy.15.offs, ...), custom_call_target="tpu_custom_call", output_to_operand_aliasing={{0}: (15, {}), {1}: (16, {})} | custom-call | flops 2147483648 | bytes 8388608 | tf_op jit(solution)/shard_map/far_slots/pallas_call | solution.py:358
  71.9 1.9 %collective-permute-done.10 = f32[2,256,256]{2,1,0:T(8,128)S(1)} collective-permute-done((f32[2,256,256]{2,1,0:T(8,128)S(1)}, f32[2,256,256]{2,1,0:T(8,128)S(1)}, u32[]{:S(2)}, u32[]{:S(2)}) %collective-permute-start.10) | collective-permute-done | bytes 524320 | tf_op jit(solution)/shard_map/ppermute | solution.py:304
  74.0 2.2 %collective-permute-start.6 = (f32[2,256,512]{2,1,0:T(8,128)}, f32[2,256,512]{2,1,0:T(8,128)S(1)}, u32[]{:S(2)}, u32[]{:S(2)}) collective-permute-start(f32[2,256,512]{2,1,0:T(8,128)} %get-tuple-element.61), channel_id=1, source_target_pairs={{0,4},{4,8},{8,12},{12,16},{16,20},{20,24},{24,28},{1,5},{5,9},{9,... | collective-permute-start | bytes 3145736 | tf_op jit(solution)/shard_map/ppermute | solution.py:21
  76.2 11.7 %collective-permute-done.11 = f32[2,256,256]{2,1,0:T(8,128)S(1)} collective-permute-done((f32[2,256,256]{2,1,0:T(8,128)S(1)}, f32[2,256,256]{2,1,0:T(8,128)S(1)}, u32[]{:S(2)}, u32[]{:S(2)}) %collective-permute-start.11) | collective-permute-done | bytes 524320 | tf_op jit(solution)/shard_map/ppermute | solution.py:304
  88.0 9.5 %collective-permute-start.12 = (f32[2,256,256]{2,1,0:T(8,128)S(1)}, f32[2,256,256]{2,1,0:T(8,128)S(1)}, u32[]{:S(2)}, u32[]{:S(2)}) collective-permute-start(f32[2,256,256]{2,1,0:T(8,128)S(1)} %add.44), channel_id=1, source_target_pairs={{0,16},{4,20},{8,24},{12,28},{16,0},{20,4},{24,8},{28,12},{1,17},{... | collective-permute-start | bytes 1572872 | tf_op jit(solution)/shard_map/ppermute | solution.py:304
  97.5 1.3 collective-permute-start.8
  98.8 16.5 %collective-permute-done.12 = f32[2,256,256]{2,1,0:T(8,128)S(1)} collective-permute-done((f32[2,256,256]{2,1,0:T(8,128)S(1)}, f32[2,256,256]{2,1,0:T(8,128)S(1)}, u32[]{:S(2)}, u32[]{:S(2)}) %collective-permute-start.12) | collective-permute-done | bytes 524320 | tf_op jit(solution)/shard_map/ppermute | solution.py:304
  115.4 7.4 %collective-permute-start.13 = (f32[2,256,256]{2,1,0:T(8,128)S(1)}, f32[2,256,256]{2,1,0:T(8,128)S(1)}, u32[]{:S(2)}, u32[]{:S(2)}) collective-permute-start(f32[2,256,256]{2,1,0:T(8,128)S(1)} %add.45), channel_id=1, source_target_pairs={{0,1},{1,0},{2,3},{3,2},{4,5},{5,4},{6,7},{7,6},{8,9},{9,8},{10,11... | collective-permute-start | bytes 1572872 | tf_op jit(solution)/shard_map/ppermute | solution.py:304
  122.8 1.9 %collective-permute-start.7 = (f32[2,256,256]{2,1,0:T(8,128)S(1)}, f32[2,256,256]{2,1,0:T(8,128)S(1)}, u32[]{:S(2)}, u32[]{:S(2)}) collective-permute-start(f32[2,256,256]{2,1,0:T(8,128)S(1)} %get-tuple-element.62), channel_id=1, source_target_pairs={{0,1},{1,2},{2,3},{4,5},{5,6},{6,7},{8,9},{9,10},{10,11},{12,13},{... | collective-permute-start | bytes 1572872 | tf_op jit(solution)/shard_map/ppermute | solution.py:21
  124.9 1.9 %collective-permute-start.9 = (f32[2,256,256]{2,1,0:T(8,128)S(1)}, f32[2,256,256]{2,1,0:T(8,128)S(1)}, u32[]{:S(2)}, u32[]{:S(2)}) collective-permute-start(f32[2,256,256]{2,1,0:T(8,128)S(1)} %add.41), channel_id=1, source_target_pairs={{0,1},{1,2},{2,3},{4,5},{5,6},{6,7},{8,9},{9,10},{10,11},{12,13},{... | collective-permute-start | bytes 1572872 | tf_op jit(solution)/shard_map/ppermute | solution.py:21
  126.8 0.3 add_dynamic-update-slice_fusion
  127.1 8.0 %collective-permute-done.13 = f32[2,256,256]{2,1,0:T(8,128)S(1)} collective-permute-done((f32[2,256,256]{2,1,0:T(8,128)S(1)}, f32[2,256,256]{2,1,0:T(8,128)S(1)}, u32[]{:S(2)}, u32[]{:S(2)}) %collective-permute-start.13) | collective-permute-done | bytes 524320 | tf_op jit(solution)/shard_map/ppermute | solution.py:304
  135.3 11.1 %collective-permute-done.7 = f32[2,256,256]{2,1,0:T(8,128)S(1)} collective-permute-done((f32[2,256,256]{2,1,0:T(8,128)S(1)}, f32[2,256,256]{2,1,0:T(8,128)S(1)}, u32[]{:S(2)}, u32[]{:S(2)}) %collective-permute-start.7) | collective-permute-done | bytes 524320 | tf_op jit(solution)/shard_map/ppermute | solution.py:21
  146.4 0.1 fusion.1
  146.5 11.1 %collective-permute-done.9 = f32[2,256,256]{2,1,0:T(8,128)S(1)} collective-permute-done((f32[2,256,256]{2,1,0:T(8,128)S(1)}, f32[2,256,256]{2,1,0:T(8,128)S(1)}, u32[]{:S(2)}, u32[]{:S(2)}) %collective-permute-start.9) | collective-permute-done | bytes 524320 | tf_op jit(solution)/shard_map/ppermute | solution.py:21
  157.6 0.1 fusion
  157.8 10.2 %collective-permute-done.14 = f32[2,256,256]{2,1,0:T(8,128)S(1)} collective-permute-done((f32[2,256,256]{2,1,0:T(8,128)S(1)}, f32[2,256,256]{2,1,0:T(8,128)S(1)}, u32[]{:S(2)}, u32[]{:S(2)}) %collective-permute-start.14) | collective-permute-done | bytes 524320 | tf_op jit(solution)/shard_map/ppermute | solution.py:304
  168.0 0.9 add_multiply_fusion
  (35 shorter events, 0.8 us)
Async XLA Ops:
  0.6 31.4 %copy-start.3 = (bf16[512,512]{1,0:T(8,128)(2,1)S(1)}, bf16[512,512]{1,0:T(8,128)(2,1)}, u32[]{:S(2)}) copy-start(bf16[512,512]{1,0:T(8,128)(2,1)} %constant.95.clone.inverse) | copy-start | bytes 1572868
  0.6 31.4 %copy-start.4 = (bf16[512,512]{1,0:T(8,128)(2,1)S(1)}, bf16[512,512]{1,0:T(8,128)(2,1)}, u32[]{:S(2)}) copy-start(bf16[512,512]{1,0:T(8,128)(2,1)} %constant.94.clone.forward) | copy-start | bytes 1572868
  0.7 11.3 %copy-start.9 = (s32[16,2]{0,1:T(2,128)S(1)}, s32[16,2]{0,1:T(2,128)}, u32[]{:S(2)}) copy-start(s32[16,2]{0,1:T(2,128)} %param.16) | copy-start | bytes 388
  0.7 31.4 %copy-start.6 = (s32[32]{0:T(128)S(1)}, s32[32]{0:T(128)}, u32[]{:S(2)}) copy-start(s32[32]{0:T(128)} %counts.5) | copy-start | bytes 388
  0.7 31.4 %copy-start.2 = (f32[2,256,256]{2,1,0:T(8,128)S(1)}, f32[2,256,256]{2,1,0:T(8,128)}, u32[]{:S(2)}) copy-start(f32[2,256,256]{2,1,0:T(8,128)} %probe.5) | copy-start | bytes 1572868
  3.1 28.9 %collective-permute-start = (f32[2,256,512]{2,1,0:T(8,128)}, f32[2,256,512]{2,1,0:T(8,128)S(1)}, u32[]{:S(2)}, u32[]{:S(2)}) collective-permute-start(f32[2,256,512]{2,1,0:T(8,128)} %slice.97), channel_id=1, source_target_pairs={{4,0},{8,4},{12,8},{16,12},{20,16},{24,20},{28,24},{5,1},{9,5},{13... | collective-permute-start | bytes 3145736 | tf_op jit(solution)/shard_map/ppermute | solution.py:21
  6.2 24.5 %collective-permute-start.1 = (f32[2,512,128]{2,1,0:T(8,128)}, f32[2,512,128]{2,1,0:T(8,128)S(1)}, u32[]{:S(2)}, u32[]{:S(2)}) collective-permute-start(f32[2,512,128]{2,1,0:T(8,128)} %slice.98), channel_id=1, source_target_pairs={{1,0},{2,1},{3,2},{5,4},{6,5},{7,6},{9,8},{10,9},{11,10},{13,12},{... | collective-permute-start | bytes 1572872 | tf_op jit(solution)/shard_map/ppermute | solution.py:21
  9.4 20.0 %collective-permute-start.3 = (f32[2,256,128]{2,1,0:T(8,128)}, f32[2,256,128]{2,1,0:T(8,128)S(1)}, u32[]{:S(2)}, u32[]{:S(2)}) collective-permute-start(f32[2,256,128]{2,1,0:T(8,128)} %get-tuple-element.67), channel_id=1, source_target_pairs={{1,0},{2,1},{3,2},{5,4},{6,5},{7,6},{9,8},{10,9},{11,10},{13,12},{... | collective-permute-start | bytes 786440 | tf_op jit(solution)/shard_map/ppermute | solution.py:21
  10.7 53.9 %collective-permute-start.4 = (f32[2,256,128]{2,1,0:T(8,128)}, f32[2,256,128]{2,1,0:T(8,128)}, u32[]{:S(2)}, u32[]{:S(2)}) collective-permute-start(f32[2,256,128]{2,1,0:T(8,128)} %get-tuple-element.66), channel_id=1, source_target_pairs={{1,0},{2,1},{3,2},{5,4},{6,5},{7,6},{9,8},{10,9},{11,10},{13,12},{... | collective-permute-start | bytes 786440 | tf_op jit(solution)/shard_map/ppermute | solution.py:21
  29.4 35.2 %collective-permute-start.5 = (f32[2,256,128]{2,1,0:T(8,128)S(1)}, f32[2,256,128]{2,1,0:T(8,128)S(1)}, u32[]{:S(2)}, u32[]{:S(2)}) collective-permute-start(f32[2,256,128]{2,1,0:T(8,128)S(1)} %collective-permute-done.3.far_top), channel_id=1, source_target_pairs={{4,0},{8,4},{12,8},{16,12},{20,16},{24,20},{28,24},{5,1},{9,5},{13... | collective-permute-start | bytes 786440 | tf_op jit(solution)/shard_map/ppermute | solution.py:21
  30.7 23.2 %collective-permute-start.2 = (f32[2,256,128]{2,1,0:T(8,128)S(1)}, f32[2,256,128]{2,1,0:T(8,128)S(1)}, u32[]{:S(2)}, u32[]{:S(2)}) collective-permute-start(f32[2,256,128]{2,1,0:T(8,128)S(1)} %slice.105), channel_id=1, source_target_pairs={{4,0},{8,4},{12,8},{16,12},{20,16},{24,20},{28,24},{5,1},{9,5},{13... | collective-permute-start | bytes 786440 | tf_op jit(solution)/shard_map/ppermute | solution.py:21
  32.1 21.8 %copy-start = (f32[2,256,512]{2,1,0:T(8,128)}, f32[2,256,512]{2,1,0:T(8,128)S(1)}, u32[]{:S(2)}) copy-start(f32[2,256,512]{2,1,0:T(8,128)S(1)} %collective-permute-done.lower_in) | copy-start | bytes 3145732
  52.7 1.1 copy-start.5
  63.6 1.0 copy-start.1
  71.8 2.0 %collective-permute-start.10 = (f32[2,256,256]{2,1,0:T(8,128)S(1)}, f32[2,256,256]{2,1,0:T(8,128)S(1)}, u32[]{:S(2)}, u32[]{:S(2)}) collective-permute-start(f32[2,256,256]{2,1,0:T(8,128)S(1)} %get-tuple-element.65), channel_id=1, source_target_pairs={{0,4},{4,0},{8,12},{12,8},{16,20},{20,16},{24,28},{28,24},{1,5},{5... | collective-permute-start | bytes 1572872 | tf_op jit(solution)/shard_map/ppermute | solution.py:304
  73.9 14.0 %collective-permute-start.11 = (f32[2,256,256]{2,1,0:T(8,128)S(1)}, f32[2,256,256]{2,1,0:T(8,128)S(1)}, u32[]{:S(2)}, u32[]{:S(2)}) collective-permute-start(f32[2,256,256]{2,1,0:T(8,128)S(1)} %add.43), channel_id=1, source_target_pairs={{0,8},{4,12},{8,0},{12,4},{16,24},{20,28},{24,16},{28,20},{1,9},{5... | collective-permute-start | bytes 1572872 | tf_op jit(solution)/shard_map/ppermute | solution.py:304
  74.0 52.9 %copy-start.7 = (f32[2,512,512]{2,1,0:T(8,128)S(1)}, f32[2,512,512]{2,1,0:T(8,128)}, u32[]{:S(2)}) copy-start(f32[2,512,512]{2,1,0:T(8,128)} %get-tuple-element.60) | copy-start | bytes 6291460
  74.0 52.9 %collective-permute-start.6 = (f32[2,256,512]{2,1,0:T(8,128)}, f32[2,256,512]{2,1,0:T(8,128)S(1)}, u32[]{:S(2)}, u32[]{:S(2)}) collective-permute-start(f32[2,256,512]{2,1,0:T(8,128)} %get-tuple-element.61), channel_id=1, source_target_pairs={{0,4},{4,8},{8,12},{12,16},{16,20},{20,24},{24,28},{1,5},{5,9},{9,... | collective-permute-start | bytes 3145736 | tf_op jit(solution)/shard_map/ppermute | solution.py:21
  88.0 27.3 %collective-permute-start.12 = (f32[2,256,256]{2,1,0:T(8,128)S(1)}, f32[2,256,256]{2,1,0:T(8,128)S(1)}, u32[]{:S(2)}, u32[]{:S(2)}) collective-permute-start(f32[2,256,256]{2,1,0:T(8,128)S(1)} %add.44), channel_id=1, source_target_pairs={{0,16},{4,20},{8,24},{12,28},{16,0},{20,4},{24,8},{28,12},{1,17},{... | collective-permute-start | bytes 1572872 | tf_op jit(solution)/shard_map/ppermute | solution.py:304
  97.5 27.3 %collective-permute-start.8 = (f32[2,256,256]{2,1,0:T(8,128)S(1)}, f32[2,256,256]{2,1,0:T(8,128)S(1)}, u32[]{:S(2)}, u32[]{:S(2)}) collective-permute-start(f32[2,256,256]{2,1,0:T(8,128)S(1)} %get-tuple-element.64), channel_id=1, source_target_pairs={{0,4},{4,8},{8,12},{12,16},{16,20},{20,24},{24,28},{1,5},{5,9},{9,... | collective-permute-start | bytes 1572872 | tf_op jit(solution)/shard_map/ppermute | solution.py:21
  115.4 19.8 %collective-permute-start.13 = (f32[2,256,256]{2,1,0:T(8,128)S(1)}, f32[2,256,256]{2,1,0:T(8,128)S(1)}, u32[]{:S(2)}, u32[]{:S(2)}) collective-permute-start(f32[2,256,256]{2,1,0:T(8,128)S(1)} %add.45), channel_id=1, source_target_pairs={{0,1},{1,0},{2,3},{3,2},{4,5},{5,4},{6,7},{7,6},{8,9},{9,8},{10,11... | collective-permute-start | bytes 1572872 | tf_op jit(solution)/shard_map/ppermute | solution.py:304
  122.8 23.5 %collective-permute-start.7 = (f32[2,256,256]{2,1,0:T(8,128)S(1)}, f32[2,256,256]{2,1,0:T(8,128)S(1)}, u32[]{:S(2)}, u32[]{:S(2)}) collective-permute-start(f32[2,256,256]{2,1,0:T(8,128)S(1)} %get-tuple-element.62), channel_id=1, source_target_pairs={{0,1},{1,2},{2,3},{4,5},{5,6},{6,7},{8,9},{9,10},{10,11},{12,13},{... | collective-permute-start | bytes 1572872 | tf_op jit(solution)/shard_map/ppermute | solution.py:21
  124.9 32.7 %collective-permute-start.9 = (f32[2,256,256]{2,1,0:T(8,128)S(1)}, f32[2,256,256]{2,1,0:T(8,128)S(1)}, u32[]{:S(2)}, u32[]{:S(2)}) collective-permute-start(f32[2,256,256]{2,1,0:T(8,128)S(1)} %add.41), channel_id=1, source_target_pairs={{0,1},{1,2},{2,3},{4,5},{5,6},{6,7},{8,9},{9,10},{10,11},{12,13},{... | collective-permute-start | bytes 1572872 | tf_op jit(solution)/shard_map/ppermute | solution.py:21
  135.2 32.7 %collective-permute-start.14 = (f32[2,256,256]{2,1,0:T(8,128)S(1)}, f32[2,256,256]{2,1,0:T(8,128)S(1)}, u32[]{:S(2)}, u32[]{:S(2)}) collective-permute-start(f32[2,256,256]{2,1,0:T(8,128)S(1)} %add.46), channel_id=1, source_target_pairs={{0,2},{1,3},{2,0},{3,1},{4,6},{5,7},{6,4},{7,5},{8,10},{9,11},{10,... | collective-permute-start | bytes 1572872 | tf_op jit(solution)/shard_map/ppermute | solution.py:304
  157.7 11.1 %copy-start.8 = (f32[2,512,512]{2,1,0:T(8,128)}, f32[2,512,512]{2,1,0:T(8,128)S(1)}, u32[]{:S(2)}) copy-start(f32[2,512,512]{2,1,0:T(8,128)S(1)} %fusion) | copy-start | bytes 6291460

commit v2 on v0

v2 whole, which is shorter than its diff:
```python
import functools
import math

import jax
import jax.numpy as jnp
import numpy as np
from jax import lax
from jax.experimental import pallas as pl
from jax.experimental.pallas import tpu as pltpu
from jax.sharding import PartitionSpec as P

LANE = 128
CHUNK = 32
PAIR = 4
VMEM_LIMIT = 28 * 1024 * 1024
F32 = jnp.float32
BF16 = jnp.bfloat16


def shifted(value, axis, steps):
    count = lax.axis_size(axis)
    leading, last = (max(0, -steps), min(count, count - steps))
    return lax.ppermute(value, axis, [(source, source + steps) for source in range(leading, last)])


def dft_blocks(window):
    index = np.arange(window)
    angle = (index[:, None] * index[None, :] % window) * (2.0 * math.pi / window)
    cosine = np.cos(angle) / math.sqrt(window)
    sine = np.sin(angle) / math.sqrt(window)
    forward = np.block([[cosine, sine], [-sine, cosine]])
    inverse = np.block([[cosine, -sine], [sine, cosine]])
    return forward.astype(BF16), inverse.astype(BF16)


def slot_steps(window, first, member, tile_cols, columns, refs):
    (offs, counts, amplitude, *tables_in, ext, acc, pacc) = refs["io"]
    (chosen, amp, patch, ext_wave, half, resid, back_half, amp_sem, *tables, table_sem) = refs["scratch"]
    (forward, inverse, probe) = tables
    loads = run_copies([
        pltpu.make_async_copy(tables_in[k], tables[k], table_sem.at[k]) for k in range(3)])
    slots = offs.shape[0]
    live = counts[lax.axis_index("row") * columns + lax.axis_index("col")]
    tile_rows = refs["tile_rows"]

    def first_tile(col):
        return lax.div(jnp.maximum(col - 1, 0), LANE)

    def pick(j, n):
        tile = first_tile(lax.rem(offs[j, 1], tile_cols))
        chosen[n] = j
        take = (j < live) & member(lax.rem(offs[j, 0], tile_rows), tile)
        return n + take.astype(jnp.int32)

    total = lax.fori_loop(0, slots, pick, jnp.int32(0))

    def fetch(i):
        buffer = lax.rem(i, 2 * PAIR)
        return pltpu.make_async_copy(
            amplitude.at[chosen[i]], amp.at[buffer], amp_sem.at[buffer])

    def fill(n):
        chosen[n] = chosen[total - 1]

    for k in range(PAIR - 1):
        @pl.when(total > 0)
        def _():
            fill(total + k)

    groups = lax.div(total + PAIR - 1, PAIR)

    @pl.when(total > 0)
    def _():
        for k in range(PAIR):
            fetch(k).start()

    refs["ready"]()
    for load in loads:
        load.wait()
    lane = lax.broadcasted_iota(jnp.int32, (CHUNK, LANE), 1)

    def body(group, carry):
        @pl.when(group + 1 < groups)
        def _():
            for k in range(PAIR):
                fetch((group + 1) * PAIR + k).start()

        places = []
        for s in range(PAIR):
            j = chosen[group * PAIR + s]
            row = lax.rem(offs[j, 0], tile_rows)
            col = lax.rem(offs[j, 1], tile_cols)
            tile = first_tile(col)
            places.append((row, tile - first, col - tile * LANE))
        for s, (row, tile, rest) in enumerate(places):
            turn = lax.rem(LANE - rest, LANE)
            head = lane < LANE - rest
            for base in range(0, window, CHUNK):
                rows = pl.ds(row + base, CHUNK)
                here = slice(base, base + CHUNK)
                planes = []
                for plane in range(2):
                    turned = [
                        pltpu.roll(ext[plane, tile + k, rows, :], turn, 1) for k in range(3)
                    ]
                    planes.append(
                        [jnp.where(head, turned[k], turned[k + 1]) for k in range(2)]
                    )
                for k in range(2):
                    cols = slice(k * LANE, (k + 1) * LANE)
                    real, imag = planes[0][k], planes[1][k]
                    patch[s, 0, here, cols] = real
                    patch[s, 1, here, cols] = imag
                    probe_real, probe_imag = probe[0, here, cols], probe[1, here, cols]
                    ext_wave[s, base : base + CHUNK, cols] = (
                        probe_real * real - probe_imag * imag
                    ).astype(BF16)
                    ext_wave[s, window + base : window + base + CHUNK, cols] = (
                        probe_real * imag + probe_imag * real
                    ).astype(BF16)
        for s in range(PAIR):
            mid = jnp.dot(forward[...], ext_wave[s], preferred_element_type=F32).astype(BF16)
            half[s, :, :window] = mid[:window]
            half[s, :, window:] = mid[window:]
        for s in range(PAIR):
            fetch(group * PAIR + s).wait()
        for s in range(PAIR):
            far = jnp.dot(half[s], inverse[...], preferred_element_type=F32)
            buffer = lax.rem(group * PAIR + s, 2 * PAIR)
            for base in range(0, window, CHUNK):
                here = slice(base, base + CHUNK)
                real, imag = far[here, :window], far[here, window:]
                level = amp[buffer, here, :].astype(F32)
                factor = 1.0 - level * lax.rsqrt(real * real + imag * imag + 0.25)
                resid[s, here, :] = (real * factor).astype(BF16)
                resid[s, window + base : window + base + CHUNK, :] = (imag * factor).astype(BF16)
        for s in range(PAIR):
            mid = jnp.dot(inverse[...], resid[s], preferred_element_type=F32).astype(BF16)
            back_half[s, :, :window] = mid[:window]
            back_half[s, :, window:] = mid[window:]
        for s, (row, tile, rest) in enumerate(places):
            back = jnp.dot(back_half[s], forward[...], preferred_element_type=F32)
            turn = lax.rem(rest, LANE)
            tail = lane >= rest
            weight = (group * PAIR + s < total).astype(F32)
            for base in range(0, window, CHUNK):
                rows = pl.ds(row + base, CHUNK)
                here = slice(base, base + CHUNK)
                terms = [[], []]
                for k in range(2):
                    cols = slice(k * LANE, (k + 1) * LANE)
                    real = back[here, k * LANE : (k + 1) * LANE]
                    imag = back[here, window + k * LANE : window + (k + 1) * LANE]
                    if s:
                        real, imag = real * weight, imag * weight
                    probe_real, probe_imag = probe[0, here, cols], probe[1, here, cols]
                    patch_real, patch_imag = patch[s, 0, here, cols], patch[s, 1, here, cols]
                    pacc[0, here, cols] += patch_real * real + patch_imag * imag
                    pacc[1, here, cols] += patch_real * imag - patch_imag * real
                    terms[0].append(pltpu.roll(probe_real * real + probe_imag * imag, turn, 1))
                    terms[1].append(pltpu.roll(probe_real * imag - probe_imag * real, turn, 1))
                for plane in range(2):
                    left, right = terms[plane]
                    acc[plane, tile, rows, :] += jnp.where(tail, left, 0.0)
                    acc[plane, tile + 1, rows, :] += jnp.where(tail, right, left)
                    acc[plane, tile + 2, rows, :] += jnp.where(tail, 0.0, right)
        return carry

    lax.fori_loop(0, groups, body, 0)


def run_copies(copies):
    for copy in copies:
        copy.start()
    return copies


def make_scratch(window, tiles, rows, copies):
    return [
        pltpu.VMEM((2, tiles, rows, LANE), F32),
        pltpu.VMEM((2, tiles, rows, LANE), F32),
        pltpu.VMEM((2, window, window), F32),
        pltpu.SMEM((32,), jnp.int32),
        pltpu.VMEM((2 * PAIR, window, window), BF16),
        pltpu.VMEM((PAIR, 2, window, window), F32),
        pltpu.VMEM((PAIR, 2 * window, window), BF16),
        pltpu.VMEM((PAIR, window, 2 * window), BF16),
        pltpu.VMEM((PAIR, 2 * window, window), BF16),
        pltpu.VMEM((PAIR, window, 2 * window), BF16),
        pltpu.SemaphoreType.DMA((2 * PAIR,)),
        pltpu.VMEM((2 * window, 2 * window), BF16),
        pltpu.VMEM((2 * window, 2 * window), BF16),
        pltpu.VMEM((2, window, window), F32),
        pltpu.SemaphoreType.DMA((3,)),
        pltpu.SemaphoreType.DMA((copies,)),
    ]


SMEM = pl.BlockSpec(memory_space=pltpu.SMEM)
VMEM = pl.BlockSpec(memory_space=pltpu.VMEM)
HBM = pl.BlockSpec(memory_space=pl.ANY)


def span(tile, count=1):
    return pl.ds(tile * LANE, count * LANE)


def slice_kernel(spots, tile_in, *refs):
    *outs, sems = refs
    copies = run_copies([
        pltpu.make_async_copy(
            tile_in.at[:, pl.ds(row, rows), pl.ds(col, cols)], outs[k], sems.at[k])
        for k, (row, rows, col, cols) in enumerate(spots)
    ])
    for copy in copies:
        copy.wait()


def slices(tile, spots, name):
    return pl.pallas_call(
        functools.partial(slice_kernel, spots),
        out_shape=[jax.ShapeDtypeStruct((2, rows, cols), F32) for _, rows, _, cols in spots],
        in_specs=[HBM],
        out_specs=[VMEM] * len(spots),
        scratch_shapes=[pltpu.SemaphoreType.DMA((len(spots),))],
        name=name,
    )(tile)


def merge_kernel(places, own_in, *refs):
    count = len(places)
    added, (own, *held), sems = refs[:count], refs[count:-1], refs[-1]
    spots = [
        own.at[:, pl.ds(row, rows), pl.ds(col, cols)] for row, rows, col, cols in places]
    loads = []
    for k in range(count):
        loads += run_copies([
            pltpu.make_async_copy(spots[k], held[2 * k], sems.at[3 * k]),
            pltpu.make_async_copy(added[k], held[2 * k + 1], sems.at[3 * k + 1]),
        ])
    stores = []
    for k in range(count):
        loads[2 * k].wait()
        loads[2 * k + 1].wait()
        held[2 * k][...] += held[2 * k + 1][...]
        stores += run_copies([pltpu.make_async_copy(held[2 * k], spots[k], sems.at[3 * k + 2])])
    for store in stores:
        store.wait()


def merge(own, blocks, places, name):
    scratch = []
    for _, rows, _, cols in places:
        scratch += [pltpu.VMEM((2, rows, cols), F32)] * 2
    return pl.pallas_call(
        functools.partial(merge_kernel, places),
        out_shape=jax.ShapeDtypeStruct(own.shape, F32),
        in_specs=[HBM] * (1 + len(blocks)),
        out_specs=HBM,
        input_output_aliases={0: 0},
        scratch_shapes=scratch + [pltpu.SemaphoreType.DMA((3 * len(blocks),))],
        compiler_params=pltpu.CompilerParams(vmem_limit_bytes=VMEM_LIMIT),
        name=name,
    )(own, *blocks)


def slots_of(shape, first, member, io, scratch, copies):
    rows, cols, window, columns = shape

    def ready():
        for copy in copies:
            copy.wait()

    slot_steps(window, first, member, cols, columns, dict(
        io=io, scratch=scratch, tile_rows=rows, ready=ready))


def inside_kernel(
    shape, offs, counts, amplitude, forward, inverse, probe, tile_in, part, probe_sum,
    ext, acc, pacc, *scratch_sems,
):
    *scratch, sems = scratch_sems
    rows, cols, window, columns = shape
    tiles = cols // LANE
    copies = run_copies([
        pltpu.make_async_copy(tile_in.at[:, :, span(k)], ext.at[:, k], sems.at[k])
        for k in range(tiles)
    ])
    acc[...] = jnp.zeros_like(acc)
    pacc[...] = jnp.zeros_like(pacc)
    slots_of(
        shape, 0, lambda row, tile: (row <= rows - window) & (tile < tiles - 2),
        (offs, counts, amplitude, forward, inverse, probe, ext, acc, pacc), scratch, copies)
    out = run_copies([
        pltpu.make_async_copy(acc, part, sems.at[0]),
        pltpu.make_async_copy(pacc, probe_sum, sems.at[1]),
    ])
    for copy in out:
        copy.wait()


def below_kernel(
    shape, offs, counts, amplitude, forward, inverse, probe, tile_in, lower_in, part, probe_in,
    own, strip, spill, probe_sum,
    ext, acc, pacc, *scratch_sems,
):
    *scratch, sems = scratch_sems
    rows, cols, window, columns = shape
    tiles = cols // LANE
    copies = [
        pltpu.make_async_copy(part, acc.at[:, :, pl.ds(0, rows), :], sems.at[2 * tiles]),
        pltpu.make_async_copy(probe_in, pacc, sems.at[2 * tiles + 1]),
    ]
    for k in range(tiles):
        copies.append(pltpu.make_async_copy(
            tile_in.at[:, :, span(k)], ext.at[:, k, pl.ds(0, rows), :], sems.at[2 * k]))
        copies.append(pltpu.make_async_copy(
            lower_in.at[:, :, span(k)], ext.at[:, k, pl.ds(rows, window), :], sems.at[2 * k + 1]))
    run_copies(copies)
    acc[:, :, rows:, :] = jnp.zeros((2, tiles, window, LANE), F32)
    slots_of(
        shape, 0, lambda row, tile: (row > rows - window) & (tile < tiles - 2),
        (offs, counts, amplitude, forward, inverse, probe, ext, acc, pacc), scratch, copies)
    out = []
    for k in range(tiles - 2):
        out.append(pltpu.make_async_copy(
            acc.at[:, k, pl.ds(0, rows), :], own.at[:, :, span(k)], sems.at[2 * k]))
        out.append(pltpu.make_async_copy(
            acc.at[:, k, pl.ds(rows, window), :], strip.at[:, :, span(k)], sems.at[2 * k + 1]))
    out.append(pltpu.make_async_copy(acc.at[:, pl.ds(tiles - 2, 2)], spill, sems.at[2 * tiles]))
    out.append(pltpu.make_async_copy(pacc, probe_sum, sems.at[2 * tiles + 1]))
    run_copies(out)
    for copy in out:
        copy.wait()


def across_kernel(
    shape, offs, counts, amplitude, forward, inverse, probe, tile_in, lower_in, top_in, bottom_in, corner_in,
    spill, probe_in, own_in, strip_in,
    own, strip, top, bottom, corner, probe_sum,
    ext, acc, pacc, *scratch_sems,
):
    *scratch, sems = scratch_sems
    rows, cols, window, columns = shape
    first = cols // LANE - 2
    copies = [
        pltpu.make_async_copy(spill, acc.at[:, pl.ds(0, 2)], sems.at[0]),
        pltpu.make_async_copy(probe_in, pacc, sems.at[1]),
    ]
    for k in range(2):
        for n, (source, start, count) in enumerate((
            (tile_in.at[:, :, span(first + k)], 0, rows),
            (lower_in.at[:, :, span(first + k)], rows, window),
        )):
            copies.append(pltpu.make_async_copy(
                source, ext.at[:, k, pl.ds(start, count), :], sems.at[2 + 5 * k + n]))
        for n, (source, start, count) in enumerate((
            (top_in, 0, window), (bottom_in, window, rows - window), (corner_in, rows, window),
        )):
            copies.append(pltpu.make_async_copy(
                source.at[:, :, span(k)], ext.at[:, 2 + k, pl.ds(start, count), :], sems.at[4 + 5 * k + n]))
    run_copies(copies)
    acc[:, 2:] = jnp.zeros_like(acc[:, 2:])
    slots_of(
        shape, first, lambda row, tile: tile >= first,
        (offs, counts, amplitude, forward, inverse, probe, ext, acc, pacc), scratch, copies)
    out = [pltpu.make_async_copy(pacc, probe_sum, sems.at[0])]
    for k in range(2):
        for n, (target, place, start, count) in enumerate((
            (own.at[:, :, span(first + k)], k, 0, rows),
            (strip.at[:, :, span(first + k)], k, rows, window),
            (top.at[:, :, span(k)], 2 + k, 0, window),
            (bottom.at[:, :, span(k)], 2 + k, window, rows - window),
            (corner.at[:, :, span(k)], 2 + k, rows, window),
        )):
            out.append(pltpu.make_async_copy(
                acc.at[:, place, pl.ds(start, count), :], target, sems.at[1 + 5 * k + n]))
    run_copies(out)
    for copy in out:
        copy.wait()


def exchange_total(value, axis):
    count = lax.axis_size(axis)
    step = 1
    while step < count:
        masks = (1, 2, 3) if 4 * step <= count else (1,)
        terms = [value] + [
            lax.ppermute(value, axis, [(k, k ^ (mask * step)) for k in range(count)]) for mask in masks
        ]
        while len(terms) > 1:
            terms = [terms[k] + terms[k + 1] for k in range(0, len(terms), 2)]
        value = terms[0]
        step *= len(masks) + 1
    return value


def per_device(object_field, illumination, amplitude, offsets, slot_counts):
    rows, cols = object_field.shape[1:]
    window = illumination.shape[1]
    slots = offsets.shape[0]
    columns = lax.axis_size("col")
    shape = (rows, cols, window, columns)
    tiles = cols // LANE
    reach = rows + window
    forward, inverse = dft_blocks(window)
    forward, inverse = jnp.asarray(forward), jnp.asarray(inverse)
    params = pltpu.CompilerParams(vmem_limit_bytes=VMEM_LIMIT)

    def sds(*dims):
        return jax.ShapeDtypeStruct(dims, F32)

    def slots_call(kernel, count, outs, extra, place, tiles_held, aliases=None):
        return pl.pallas_call(
            functools.partial(kernel, shape),
            out_shape=[sds(*dims) for dims in outs],
            in_specs=[SMEM, SMEM] + [HBM] * (4 + len(extra)),
            out_specs=[HBM] * len(outs),
            input_output_aliases=aliases or {},
            scratch_shapes=make_scratch(window, tiles_held, place, 12),
            compiler_params=params,
            cost_estimate=pl.CostEstimate(
                flops=32 * window**3 * count, bytes_accessed=8 * 2**20, transcendentals=0),
            name=kernel.__name__,
        )(offsets, slot_counts, amplitude, forward, inverse, illumination, *extra)

    plane = (2, window, window)
    (top_own,) = slices(object_field, ((0, window, 0, window),), "slice_top")
    tile, top_own = lax.optimization_barrier((object_field, top_own))
    bottom_own, lower_own = slices(
        tile, ((window, rows - window, 0, window), (0, window, 0, cols)), "slice_rest")
    top_right = shifted(top_own, "col", -1)
    lower = shifted(lower_own, "row", -1)
    bottom_right = shifted(bottom_own, "col", -1)
    part, probe_sum = slots_call(
        inside_kernel, 8, [(2, tiles, rows, LANE), plane], (object_field,), rows, tiles)
    top_right, part = lax.optimization_barrier((top_right, part))
    corner_right = shifted(top_right, "row", -1)
    own, strip, spill, probe_sum = slots_call(
        below_kernel, 8, [(2, rows, cols), (2, window, cols), (2, 2, reach, LANE), plane],
        (object_field, lower, part, probe_sum), reach, tiles)
    own, strip, top, bottom, corner, probe_sum = slots_call(
        across_kernel, 8,
        [(2, rows, cols), (2, window, cols), plane, (2, rows - window, window), plane, plane],
        (object_field, lower, top_right, bottom_right, corner_right, spill, probe_sum, own, strip),
        reach, 4, {13: 0, 14: 1})

    corner_back = shifted(corner, "row", 1)
    bottom_back = shifted(bottom, "col", 1)
    pieces = lax.axis_size("row")
    scattered = lax.all_to_all(
        probe_sum.reshape(pieces, -1, window), "row", 0, 0, tiled=True)
    scattered, corner_back, bottom_back, strip = lax.optimization_barrier(
        (scattered, corner_back, bottom_back, strip))
    top_back = shifted(top + corner_back, "col", 1)
    strip_back = shifted(strip, "row", 1)
    piece = exchange_total(jnp.sum(scattered, axis=0), "col")
    summed = lax.all_gather(piece, "row").reshape(plane)
    own = merge(own, (strip_back, bottom_back),
                ((0, window, 0, cols), (window, rows - window, 0, window)), "first_merge")
    own = merge(own, (top_back,), ((0, window, 0, window),), "last_merge")
    live_total = slots * lax.axis_size("row") * lax.axis_size("col") // 2
    return own, summed * (1.0 / math.sqrt(live_total))


def solution(mesh):
    return jax.shard_map(
        per_device,
        mesh=mesh,
        in_specs=(
            P(None, "row", "col"),
            P(),
            P(("row", "col"), None, None),
            P(("row", "col"), None),
            P(),
        ),
        out_specs=(P(None, "row", "col"), P()),
        check_vma=False,
    )
```

time: 592 us -> 101 us (0.17); the launches traced: 586 us -> 102 us
  local copies, waits for them, and re-layouts: 196 us -> 4.82 us
  waiting for transfers between devices: 172 us -> 9.27 us
  loops' own time: 84.8 us -> 0 us
  matrix products: 64.5 us -> 0 us
  other arithmetic: 39.9 us -> 0.95 us
  blocking collectives: 0 us -> 36.1 us
  Pallas kernels: 0 us -> 31.2 us
  between operations: 14.2 us -> 1.01 us
    psum x1 -> x0, waiting for transfers between devices: 145 us -> none  [per_device(): summed = lax.psum(probe_total, ('row', 'col'))]
    dynamic_update_slice x16 -> x0, local copies, waits for them, and re-layouts: 92.9 us -> none  [add_patch(): lax.dynamic_update_slice(current, block + spread, (zero_index, corner_row...]
    another operation x2 -> x0, loops' own time: 84.8 us -> none  [the longest x1 84.8 us: per_device(): accumulated = lax.fori_loop(0, slots, add_slot, accumulated)]
    gather x48 -> x0, local copies, waits for them, and re-layouts: 69.6 us -> none
    dot_general x19 -> x0, matrix products: 64.5 us -> none  [the longest x16 30.8 us: add_patch(): jnp.einsum('crw,kw->crk', terms, table, precision=lax.Precision.HIGHEST)]
    pallas_call x0 -> x7, Pallas kernels: none -> 31.2 us  [the longest x3 22.2 us: slots_call(): pl.pallas_call(functools.partial(kernel, shape), out_shape=[sds(*dims) fo...]
    all_to_all x0 -> x1, blocking collectives: none -> 24.7 us  [per_device(): lax.all_to_all(probe_sum.reshape(pieces, -1, window), 'row', 0, 0, tiled=...]
    ppermute x4 -> x8, waiting for transfers between devices: 26.8 us -> 6.95 us  [shifted(): lax.ppermute(value, axis, [(source, source + steps) for source in range(l...]
  transfers between devices with their start and end apart: 5 -> 11, of which waited for: 3 -> 4; matrix products, arithmetic and copies ran while one was open for 3% -> 1% of each run, Pallas kernels for 0% -> 16%
where the time goes in v2:
time: 101 us; the launch traced here: 102 us
  blocking collectives  36.1 us (36%)
  Pallas kernels  31.2 us (31%)
  starting transfers between devices  19 us (19%)
  waiting for transfers between devices  9.27 us (9%)
  local copies, waits for them, and re-layouts  4.82 us (5%)
  between operations  1.01 us (1%)
    all_to_all x1, blocking collectives, per_device(): lax.all_to_all(probe_sum.reshape(pieces, -1, window), 'row', 0, 0, tiled=...  24.7 us
    pallas_call x3, Pallas kernels, slots_call(): pl.pallas_call(functools.partial(kernel, shape), out_shape=[sds(*dims) fo...  22.2 us
    ppermute x8, starting transfers between devices, shifted(): lax.ppermute(value, axis, [(source, source + steps) for source in range(l...  14.6 us
    all_gather x1, blocking collectives, per_device(): summed = lax.all_gather(piece, 'row').reshape(plane)  11.4 us
    ppermute x8, waiting for transfers between devices, shifted(): lax.ppermute(value, axis, [(source, source + steps) for source in range(l...  6.95 us
    unnamed x19, local copies, waits for them, and re-layouts  4.82 us
    pallas_call x2, Pallas kernels, slices(): pl.pallas_call(functools.partial(slice_kernel, spots), out_shape=[jax.Sha...  4.57 us
    pallas_call x2, Pallas kernels, merge(): pl.pallas_call(functools.partial(merge_kernel, places), out_shape=jax.Sha...  4.45 us
  transfers between devices with their start and end apart: 11, of which 4 were waited for; matrix products, arithmetic and copies ran while one was open for 1% of the time, Pallas kernels for 16%

profile of v2, /device:TPU:0, one launch (start us, length us, event | category | flops | bytes accessed | tf_op | source)
XLA Modules:
  0.0 102.4 jit_solution(5234427032571301141)
XLA Ops:
  0.6 0.0 copy-start
  0.7 2.0 %slice_top.1 = f32[2,256,256]{2,1,0:T(8,128)} custom-call(f32[2,512,512]{2,1,0:T(8,128)} %tile_in.8), custom_call_target="tpu_custom_call" | custom-call | tf_op jit(solution)/shard_map/slice_top/pallas_call | solution.py:220
  2.7 2.6 %slice_rest.1 = (f32[2,256,256]{2,1,0:T(8,128)}, f32[2,256,512]{2,1,0:T(8,128)}) custom-call(f32[2,512,512]{2,1,0:T(8,128)} %tile_in.8), custom_call_target="tpu_custom_call" | custom-call | tf_op jit(solution)/shard_map/slice_rest/pallas_call | solution.py:220
  5.3 1.3 %collective-permute-start = (f32[2,256,512]{2,1,0:T(8,128)}, f32[2,256,512]{2,1,0:T(8,128)}, u32[]{:S(2)}, u32[]{:S(2)}) collective-permute-start(f32[2,256,512]{2,1,0:T(8,128)} %get-tuple-element.25), channel_id=1, source_target_pairs={{4,0},{8,4},{12,8},{16,12},{20,16},{24,20},{28,24},{5,1},{9,5},{13... | collective-permute-start | bytes 3145736 | tf_op jit(solution)/shard_map/ppermute | solution.py:23
  6.6 1.3 %collective-permute-start.1 = (f32[2,256,256]{2,1,0:T(8,128)}, f32[2,256,256]{2,1,0:T(8,128)S(1)}, u32[]{:S(2)}, u32[]{:S(2)}) collective-permute-start(f32[2,256,256]{2,1,0:T(8,128)} %slice_top.1), channel_id=1, source_target_pairs={{1,0},{2,1},{3,2},{5,4},{6,5},{7,6},{9,8},{10,9},{11,10},{13,12},{... | collective-permute-start | bytes 1572872 | tf_op jit(solution)/shard_map/ppermute | solution.py:23
  7.9 1.3 %collective-permute-start.2 = (f32[2,256,256]{2,1,0:T(8,128)}, f32[2,256,256]{2,1,0:T(8,128)}, u32[]{:S(2)}, u32[]{:S(2)}) collective-permute-start(f32[2,256,256]{2,1,0:T(8,128)} %get-tuple-element.29), channel_id=1, source_target_pairs={{1,0},{2,1},{3,2},{5,4},{6,5},{7,6},{9,8},{10,9},{11,10},{13,12},{... | collective-permute-start | bytes 1572872 | tf_op jit(solution)/shard_map/ppermute | solution.py:23
  9.2 0.1 copy.15.offs
  9.3 1.6 %copy-done.1 = bf16[16,256,256]{2,1,0:T(8,128)(2,1)S(1)} copy-done((bf16[16,256,256]{2,1,0:T(8,128)(2,1)S(1)}, bf16[16,256,256]{2,1,0:T(8,128)(2,1)}, u32[]{:S(2)}) %copy-start.1) | copy-done | bytes 2097176
  10.9 1.0 %copy-done.6 = bf16[512,512]{1,0:T(8,128)(2,1)S(1)} copy-done((bf16[512,512]{1,0:T(8,128)(2,1)S(1)}, bf16[512,512]{1,0:T(8,128)(2,1)}, u32[]{:S(2)}) %copy-start.6) | copy-done | bytes 524312
  11.9 1.0 %copy-done.7 = bf16[512,512]{1,0:T(8,128)(2,1)S(1)} copy-done((bf16[512,512]{1,0:T(8,128)(2,1)S(1)}, bf16[512,512]{1,0:T(8,128)(2,1)}, u32[]{:S(2)}) %copy-start.7) | copy-done | bytes 524312
  12.9 6.6 %inside_kernel.1 = (f32[2,4,512,128]{3,2,1,0:T(8,128)S(1)}, f32[2,256,256]{2,1,0:T(8,128)S(1)}) custom-call(s32[16,2]{1,0:T(8,128)S(1)} %copy.15.offs, s32[32]{0:T(128)S(1)} %copy-done.5, bf16[16,256,256]{2,1,0:T(8,128)(2,1)S(1)} %copy-done.1, bf16[512,512]{1,0:T(8,128)(2,1)S(1)} %copy-done.7, bf16[512,512]{1,0:T(8,128)(2,1)S(1)} %copy-done.6, ...), custom_call_target="tpu_custom_call" | custom-call | flops 4294967296 | bytes 8388608 | tf_op jit(solution)/shard_map/inside_kernel/pallas_call | solution.py:414
  19.6 4.6 %collective-permute-done.1.top_in = f32[2,256,256]{2,1,0:T(8,128)S(1)} collective-permute-done((f32[2,256,256]{2,1,0:T(8,128)}, f32[2,256,256]{2,1,0:T(8,128)S(1)}, u32[]{:S(2)}, u32[]{:S(2)}) %collective-permute-start.1) | collective-permute-done | bytes 524320 | tf_op jit(solution)/shard_map/ppermute | solution.py:23
  24.1 1.3 %collective-permute-start.3 = (f32[2,256,256]{2,1,0:T(8,128)S(1)}, f32[2,256,256]{2,1,0:T(8,128)S(1)}, u32[]{:S(2)}, u32[]{:S(2)}) collective-permute-start(f32[2,256,256]{2,1,0:T(8,128)S(1)} %collective-permute-done.1.top_in), channel_id=1, source_target_pairs={{4,0},{8,4},{12,8},{16,12},{20,16},{24,20},{28,24},{5,1},{9,5},{13... | collective-permute-start | bytes 1572872 | tf_op jit(solution)/shard_map/ppermute | solution.py:23
  25.4 7.6 %below_kernel.1 = (f32[2,512,512]{2,1,0:T(8,128)}, f32[2,256,512]{2,1,0:T(8,128)}, f32[2,2,768,128]{3,2,1,0:T(8,128)S(1)}, f32[2,256,256]{2,1,0:T(8,128)S(1)}) custom-call(s32[16,2]{1,0:T(8,128)S(1)} %copy.15.offs, s32[32]{0:T(128)S(1)} %copy-done.5, bf16[16,256,256]{2,1,0:T(8,128)(2,1)S(1)} %copy-done.1, bf16[512,512]{1,0:T(8,128)(2,1)S(1)} %copy-done.7, ...), custom_call_target="tpu_custom_call" | custom-call | flops 4294967296 | bytes 8388608 | tf_op jit(solution)/shard_map/below_kernel/pallas_call | solution.py:414
  33.1 2.4 %collective-permute-done.2.bottom_in = f32[2,256,256]{2,1,0:T(8,128)} collective-permute-done((f32[2,256,256]{2,1,0:T(8,128)}, f32[2,256,256]{2,1,0:T(8,128)}, u32[]{:S(2)}, u32[]{:S(2)}) %collective-permute-start.2) | collective-permute-done | bytes 524320 | tf_op jit(solution)/shard_map/ppermute | solution.py:23
  35.5 1.0 %copy-done.4 = f32[2,256,256]{2,1,0:T(8,128)S(1)} copy-done((f32[2,256,256]{2,1,0:T(8,128)S(1)}, f32[2,256,256]{2,1,0:T(8,128)}, u32[]{:S(2)}) %copy-start.4) | copy-done | bytes 524312
  36.5 7.9 %across_kernel.1 = (f32[2,512,512]{2,1,0:T(8,128)}, f32[2,256,512]{2,1,0:T(8,128)}, f32[2,256,256]{2,1,0:T(8,128)S(1)}, f32[2,256,256]{2,1,0:T(8,128)S(1)}, f32[...) custom-call(s32[16,2]{1,0:T(8,128)S(1)} %copy.15.offs, ...), custom_call_target="tpu_custom_call", output_to_operand_aliasing={{0}: (13, {}), {1}: (14, {})} | custom-call | flops 4294967296 | bytes 8388608 | tf_op jit(solution)/shard_map/across_kernel/pallas_call | solution.py:414
  44.4 2.3 %collective-permute-start.4 = (f32[2,256,256]{2,1,0:T(8,128)S(1)}, f32[2,256,256]{2,1,0:T(8,128)S(1)}, u32[]{:S(2)}, u32[]{:S(2)}) collective-permute-start(f32[2,256,256]{2,1,0:T(8,128)S(1)} %get-tuple-element.38), channel_id=1, source_target_pairs={{0,4},{4,8},{8,12},{12,16},{16,20},{20,24},{24,28},{1,5},{5,9},{9,... | collective-permute-start | bytes 1572872 | tf_op jit(solution)/shard_map/ppermute | solution.py:23
  46.7 3.9 %collective-permute-start.5 = (f32[2,256,256]{2,1,0:T(8,128)S(1)}, f32[2,256,256]{2,1,0:T(8,128)S(1)}, u32[]{:S(2)}, u32[]{:S(2)}) collective-permute-start(f32[2,256,256]{2,1,0:T(8,128)S(1)} %get-tuple-element.39), channel_id=1, source_target_pairs={{0,1},{1,2},{2,3},{4,5},{5,6},{6,7},{8,9},{9,10},{10,11},{12,13},{... | collective-permute-start | bytes 1572872 | tf_op jit(solution)/shard_map/ppermute | solution.py:23
  50.6 24.7 %all_to_all.5 = f32[8,64,256]{2,1,0:T(8,128)S(1)} all-to-all(f32[8,64,256]{2,1,0:T(8,128)S(1)} %bitcast.2), channel_id=1, replica_groups=mesh['row'=8,'col'=4] {'row'}, dimensions={0} | all-to-all | bytes 1048576 | tf_op jit(solution)/shard_map/all_to_all | solution.py:451
  75.3 1.3 %collective-permute-start.6 = (f32[2,256,512]{2,1,0:T(8,128)}, f32[2,256,512]{2,1,0:T(8,128)S(1)}, u32[]{:S(2)}, u32[]{:S(2)}) collective-permute-start(f32[2,256,512]{2,1,0:T(8,128)} %get-tuple-element.41), channel_id=1, source_target_pairs={{0,4},{4,8},{8,12},{12,16},{16,20},{20,24},{24,28},{1,5},{5,9},{9,... | collective-permute-start | bytes 3145736 | tf_op jit(solution)/shard_map/ppermute | solution.py:23
  76.7 0.1 collective-permute-start.10
  76.8 1.7 %collective-permute-start.9 = (f32[64,256]{1,0:T(8,128)S(1)}, f32[64,256]{1,0:T(8,128)S(1)}, u32[]{:S(2)}, u32[]{:S(2)}) collective-permute-start(f32[64,256]{1,0:T(8,128)S(1)} %reduce_sum.9), channel_id=1, source_target_pairs={{0,2},{1,3},{2,0},{3,1},{4,6},{5,7},{6,4},{7,5},{8,10},{9,11},{10,... | collective-permute-start | bytes 196616 | tf_op jit(solution)/shard_map/ppermute | solution.py:389
  78.5 2.7 %collective-permute-start.8 = (f32[64,256]{1,0:T(8,128)S(1)}, f32[64,256]{1,0:T(8,128)S(1)}, u32[]{:S(2)}, u32[]{:S(2)}) collective-permute-start(f32[64,256]{1,0:T(8,128)S(1)} %reduce_sum.9), channel_id=1, source_target_pairs={{0,1},{1,0},{2,3},{3,2},{4,5},{5,4},{6,7},{7,6},{8,9},{9,8},{10,11... | collective-permute-start | bytes 196616 | tf_op jit(solution)/shard_map/ppermute | solution.py:389
  81.1 0.1 add.12
  81.2 1.9 %collective-permute-start.7 = (f32[2,256,256]{2,1,0:T(8,128)S(1)}, f32[2,256,256]{2,1,0:T(8,128)S(1)}, u32[]{:S(2)}, u32[]{:S(2)}) collective-permute-start(f32[2,256,256]{2,1,0:T(8,128)S(1)} %add.12), channel_id=1, source_target_pairs={{0,1},{1,2},{2,3},{4,5},{5,6},{6,7},{8,9},{9,10},{10,11},{12,13},{... | collective-permute-start | bytes 1572872 | tf_op jit(solution)/shard_map/ppermute | solution.py:23
  83.2 0.3 collective-permute-done.10
  83.4 2.1 %collective-permute-done.9 = f32[64,256]{1,0:T(8,128)S(1)} collective-permute-done((f32[64,256]{1,0:T(8,128)S(1)}, f32[64,256]{1,0:T(8,128)S(1)}, u32[]{:S(2)}, u32[]{:S(2)}) %collective-permute-start.9) | collective-permute-done | bytes 65568 | tf_op jit(solution)/shard_map/ppermute | solution.py:389
  85.5 11.4 %all-gather = f32[512,256]{1,0:T(8,128)S(1)} all-gather(f32[64,256]{1,0:T(8,128)S(1)} %add_add_fusion), channel_id=2, replica_groups=mesh['row'=8,'col'=4] {'row'}, dimensions={0}, use_global_device_ids=true | all-gather | bytes 589824 | tf_op jit(solution)/shard_map/all_gather | solution.py:458
  96.9 0.8 broadcast_multiply_fusion
  97.7 2.5 %first_merge.1.own_in = f32[2,512,512]{2,1,0:T(8,128)} custom-call(f32[2,512,512]{2,1,0:T(8,128)} %get-tuple-element.36.own_in, f32[2,256,512]{2,1,0:T(8,128)S(1)} %collective-permute-done.6.refs_0_, f32[2,256,256]{2,1,0:T(8,128)S(1)} %collective-permute-done.5.refs_1_), custom_call_target="tpu_custom_call", output_to_operand_aliasing={{}: (0, {})} | custom-call | tf_op jit(solution)/shard_map/first_merge/pallas_call | solution.py:255
  100.3 1.9 %last_merge.1 = f32[2,512,512]{2,1,0:T(8,128)} custom-call(f32[2,512,512]{2,1,0:T(8,128)} %first_merge.1.own_in, f32[2,256,256]{2,1,0:T(8,128)S(1)} %collective-permute-done.7.refs_0_), custom_call_target="tpu_custom_call", output_to_operand_aliasing={{}: (0, {})} | custom-call | tf_op jit(solution)/shard_map/last_merge/pallas_call | solution.py:255
  (22 shorter events, 0.1 us)
Async XLA Ops:
  0.6 8.6 %copy-start = (f32[2,512,512]{2,1,0:T(8,128)S(1)}, f32[2,512,512]{2,1,0:T(8,128)}, u32[]{:S(2)}) copy-start(f32[2,512,512]{2,1,0:T(8,128)} %tile_in.8) | copy-start | bytes 6291460
  0.6 8.5 %copy-start.8 = (s32[16,2]{0,1:T(2,128)S(1)}, s32[16,2]{0,1:T(2,128)}, u32[]{:S(2)}) copy-start(s32[16,2]{0,1:T(2,128)} %param.10) | copy-start | bytes 388
  0.7 8.6 %copy-start.5 = (s32[32]{0:T(128)S(1)}, s32[32]{0:T(128)}, u32[]{:S(2)}) copy-start(s32[32]{0:T(128)} %counts.5) | copy-start | bytes 388
  0.7 8.6 %copy-start.2 = (f32[2,256,256]{2,1,0:T(8,128)S(1)}, f32[2,256,256]{2,1,0:T(8,128)}, u32[]{:S(2)}) copy-start(f32[2,256,256]{2,1,0:T(8,128)} %probe.5) | copy-start | bytes 1572868
  5.3 20.1 %collective-permute-start = (f32[2,256,512]{2,1,0:T(8,128)}, f32[2,256,512]{2,1,0:T(8,128)}, u32[]{:S(2)}, u32[]{:S(2)}) collective-permute-start(f32[2,256,512]{2,1,0:T(8,128)} %get-tuple-element.25), channel_id=1, source_target_pairs={{4,0},{8,4},{12,8},{16,12},{20,16},{24,20},{28,24},{5,1},{9,5},{13... | collective-permute-start | bytes 3145736 | tf_op jit(solution)/shard_map/ppermute | solution.py:23
  6.6 17.6 %collective-permute-start.1 = (f32[2,256,256]{2,1,0:T(8,128)}, f32[2,256,256]{2,1,0:T(8,128)S(1)}, u32[]{:S(2)}, u32[]{:S(2)}) collective-permute-start(f32[2,256,256]{2,1,0:T(8,128)} %slice_top.1), channel_id=1, source_target_pairs={{1,0},{2,1},{3,2},{5,4},{6,5},{7,6},{9,8},{10,9},{11,10},{13,12},{... | collective-permute-start | bytes 1572872 | tf_op jit(solution)/shard_map/ppermute | solution.py:23
  7.9 27.6 %collective-permute-start.2 = (f32[2,256,256]{2,1,0:T(8,128)}, f32[2,256,256]{2,1,0:T(8,128)}, u32[]{:S(2)}, u32[]{:S(2)}) collective-permute-start(f32[2,256,256]{2,1,0:T(8,128)} %get-tuple-element.29), channel_id=1, source_target_pairs={{1,0},{2,1},{3,2},{5,4},{6,5},{7,6},{9,8},{10,9},{11,10},{13,12},{... | collective-permute-start | bytes 1572872 | tf_op jit(solution)/shard_map/ppermute | solution.py:23
  9.3 1.6 %copy-start.1 = (bf16[16,256,256]{2,1,0:T(8,128)(2,1)S(1)}, bf16[16,256,256]{2,1,0:T(8,128)(2,1)}, u32[]{:S(2)}) copy-start(bf16[16,256,256]{2,1,0:T(8,128)(2,1)} %amplitude.5) | copy-start | bytes 6291460
  10.9 1.0 %copy-start.6 = (bf16[512,512]{1,0:T(8,128)(2,1)S(1)}, bf16[512,512]{1,0:T(8,128)(2,1)}, u32[]{:S(2)}) copy-start(bf16[512,512]{1,0:T(8,128)(2,1)} %constant.9.clone.inverse) | copy-start | bytes 1572868
  11.9 1.0 %copy-start.7 = (bf16[512,512]{1,0:T(8,128)(2,1)S(1)}, bf16[512,512]{1,0:T(8,128)(2,1)}, u32[]{:S(2)}) copy-start(bf16[512,512]{1,0:T(8,128)(2,1)} %constant.8.clone.forward) | copy-start | bytes 1572868
  24.1 9.0 %copy-start.3 = (f32[2,256,256]{2,1,0:T(8,128)}, f32[2,256,256]{2,1,0:T(8,128)S(1)}, u32[]{:S(2)}) copy-start(f32[2,256,256]{2,1,0:T(8,128)S(1)} %collective-permute-done.1.top_in) | copy-start | bytes 1572868
  24.1 11.3 %collective-permute-start.3 = (f32[2,256,256]{2,1,0:T(8,128)S(1)}, f32[2,256,256]{2,1,0:T(8,128)S(1)}, u32[]{:S(2)}, u32[]{:S(2)}) collective-permute-start(f32[2,256,256]{2,1,0:T(8,128)S(1)} %collective-permute-done.1.top_in), channel_id=1, source_target_pairs={{4,0},{8,4},{12,8},{16,12},{20,16},{24,20},{28,24},{5,1},{9,5},{13... | collective-permute-start | bytes 1572872 | tf_op jit(solution)/shard_map/ppermute | solution.py:23
  35.5 1.0 %copy-start.4 = (f32[2,256,256]{2,1,0:T(8,128)S(1)}, f32[2,256,256]{2,1,0:T(8,128)}, u32[]{:S(2)}) copy-start(f32[2,256,256]{2,1,0:T(8,128)} %copy-done.3) | copy-start | bytes 1572868
  44.4 30.8 %collective-permute-start.4 = (f32[2,256,256]{2,1,0:T(8,128)S(1)}, f32[2,256,256]{2,1,0:T(8,128)S(1)}, u32[]{:S(2)}, u32[]{:S(2)}) collective-permute-start(f32[2,256,256]{2,1,0:T(8,128)S(1)} %get-tuple-element.38), channel_id=1, source_target_pairs={{0,4},{4,8},{8,12},{12,16},{16,20},{20,24},{24,28},{1,5},{5,9},{9,... | collective-permute-start | bytes 1572872 | tf_op jit(solution)/shard_map/ppermute | solution.py:23
  46.7 28.6 %collective-permute-start.5 = (f32[2,256,256]{2,1,0:T(8,128)S(1)}, f32[2,256,256]{2,1,0:T(8,128)S(1)}, u32[]{:S(2)}, u32[]{:S(2)}) collective-permute-start(f32[2,256,256]{2,1,0:T(8,128)S(1)} %get-tuple-element.39), channel_id=1, source_target_pairs={{0,1},{1,2},{2,3},{4,5},{5,6},{6,7},{8,9},{9,10},{10,11},{12,13},{... | collective-permute-start | bytes 1572872 | tf_op jit(solution)/shard_map/ppermute | solution.py:23
  75.3 22.5 %collective-permute-start.6 = (f32[2,256,512]{2,1,0:T(8,128)}, f32[2,256,512]{2,1,0:T(8,128)S(1)}, u32[]{:S(2)}, u32[]{:S(2)}) collective-permute-start(f32[2,256,512]{2,1,0:T(8,128)} %get-tuple-element.41), channel_id=1, source_target_pairs={{0,4},{4,8},{8,12},{12,16},{16,20},{20,24},{24,28},{1,5},{5,9},{9,... | collective-permute-start | bytes 3145736 | tf_op jit(solution)/shard_map/ppermute | solution.py:23
  76.7 6.7 %collective-permute-start.10 = (f32[64,256]{1,0:T(8,128)S(1)}, f32[64,256]{1,0:T(8,128)S(1)}, u32[]{:S(2)}, u32[]{:S(2)}) collective-permute-start(f32[64,256]{1,0:T(8,128)S(1)} %reduce_sum.9), channel_id=1, source_target_pairs={{0,3},{1,2},{2,1},{3,0},{4,7},{5,6},{6,5},{7,4},{8,11},{9,10},{10,... | collective-permute-start | bytes 196616 | tf_op jit(solution)/shard_map/ppermute | solution.py:389
  76.8 8.7 %collective-permute-start.9 = (f32[64,256]{1,0:T(8,128)S(1)}, f32[64,256]{1,0:T(8,128)S(1)}, u32[]{:S(2)}, u32[]{:S(2)}) collective-permute-start(f32[64,256]{1,0:T(8,128)S(1)} %reduce_sum.9), channel_id=1, source_target_pairs={{0,2},{1,3},{2,0},{3,1},{4,6},{5,7},{6,4},{7,5},{8,10},{9,11},{10,... | collective-permute-start | bytes 196616 | tf_op jit(solution)/shard_map/ppermute | solution.py:389
  78.5 7.0 %collective-permute-start.8 = (f32[64,256]{1,0:T(8,128)S(1)}, f32[64,256]{1,0:T(8,128)S(1)}, u32[]{:S(2)}, u32[]{:S(2)}) collective-permute-start(f32[64,256]{1,0:T(8,128)S(1)} %reduce_sum.9), channel_id=1, source_target_pairs={{0,1},{1,0},{2,3},{3,2},{4,5},{5,4},{6,7},{7,6},{8,9},{9,8},{10,11... | collective-permute-start | bytes 196616 | tf_op jit(solution)/shard_map/ppermute | solution.py:389
  81.2 19.1 %collective-permute-start.7 = (f32[2,256,256]{2,1,0:T(8,128)S(1)}, f32[2,256,256]{2,1,0:T(8,128)S(1)}, u32[]{:S(2)}, u32[]{:S(2)}) collective-permute-start(f32[2,256,256]{2,1,0:T(8,128)S(1)} %add.12), channel_id=1, source_target_pairs={{0,1},{1,2},{2,3},{4,5},{5,6},{6,7},{8,9},{9,10},{10,11},{12,13},{... | collective-permute-start | bytes 1572872 | tf_op jit(solution)/shard_map/ppermute | solution.py:23

commit v3 on v2

--- a/solution.py
+++ b/solution.py
@@ -59,45 +59,46 @@
         return pltpu.make_async_copy(
             amplitude.at[chosen[i]], amp.at[buffer], amp_sem.at[buffer])
 
-    def fill(n):
-        chosen[n] = chosen[total - 1]
+    whole = lax.div(total, PAIR)
+    left_over = total - whole * PAIR
+    half_group = (left_over > 0) & (left_over <= PAIR // 2)
+    full_groups = whole + (left_over > PAIR // 2).astype(jnp.int32)
+    padded = full_groups * PAIR + half_group.astype(jnp.int32) * (PAIR // 2)
 
     for k in range(PAIR - 1):
         @pl.when(total > 0)
         def _():
-            fill(total + k)
-
-    groups = lax.div(total + PAIR - 1, PAIR)
-
-    @pl.when(total > 0)
-    def _():
+            chosen[total + k] = chosen[total - 1]
+
+    def fetch_from(base):
         for k in range(PAIR):
-            fetch(k).start()
+            @pl.when(base + k < padded)
+            def _():
+                fetch(base + k).start()
+
+    fetch_from(0)
 
     refs["ready"]()
     for load in loads:
         load.wait()
     lane = lax.broadcasted_iota(jnp.int32, (CHUNK, LANE), 1)
 
-    def body(group, carry):
-        @pl.when(group + 1 < groups)
-        def _():
-            for k in range(PAIR):
-                fetch((group + 1) * PAIR + k).start()
-
+    def body(base, size):
+        fetch_from(base + size)
         places = []
-        for s in range(PAIR):
-            j = chosen[group * PAIR + s]
+        for s in range(size):
+            j = chosen[base + s]
             row = lax.rem(offs[j, 0], tile_rows)
             col = lax.rem(offs[j, 1], tile_cols)
             tile = first_tile(col)
             places.append((row, tile - first, col - tile * LANE))
-        for s, (row, tile, rest) in enumerate(places):
+        def extract(s):
+            row, tile, rest = places[s]
             turn = lax.rem(LANE - rest, LANE)
             head = lane < LANE - rest
-            for base in range(0, window, CHUNK):
-                rows = pl.ds(row + base, CHUNK)
-                here = slice(base, base + CHUNK)
+            for line in range(0, window, CHUNK):
+                rows = pl.ds(row + line, CHUNK)
+                here = slice(line, line + CHUNK)
                 planes = []
                 for plane in range(2):
                     turned = [
@@ -112,40 +113,51 @@
                     patch[s, 0, here, cols] = real
                     patch[s, 1, here, cols] = imag
                     probe_real, probe_imag = probe[0, here, cols], probe[1, here, cols]
-                    ext_wave[s, base : base + CHUNK, cols] = (
+                    ext_wave[s, line : line + CHUNK, cols] = (
                         probe_real * real - probe_imag * imag
                     ).astype(BF16)
-                    ext_wave[s, window + base : window + base + CHUNK, cols] = (
+                    ext_wave[s, window + line : window + line + CHUNK, cols] = (
                         probe_real * imag + probe_imag * real
                     ).astype(BF16)
-        for s in range(PAIR):
-            mid = jnp.dot(forward[...], ext_wave[s], preferred_element_type=F32).astype(BF16)
-            half[s, :, :window] = mid[:window]
-            half[s, :, window:] = mid[window:]
-        for s in range(PAIR):
-            fetch(group * PAIR + s).wait()
-        for s in range(PAIR):
+                yield
+
+        def rows_forward(s):
+            for n in range(2):
+                part = slice(n * window, (n + 1) * window)
+                half[s, :, part] = jnp.dot(
+                    forward[part, :], ext_wave[s], preferred_element_type=F32).astype(BF16)
+                yield
+
+        def columns_forward(s):
             far = jnp.dot(half[s], inverse[...], preferred_element_type=F32)
-            buffer = lax.rem(group * PAIR + s, 2 * PAIR)
-            for base in range(0, window, CHUNK):
-                here = slice(base, base + CHUNK)
+            yield
+            buffer = lax.rem(base + s, 2 * PAIR)
+            for line in range(0, window, CHUNK):
+                here = slice(line, line + CHUNK)
                 real, imag = far[here, :window], far[here, window:]
                 level = amp[buffer, here, :].astype(F32)
                 factor = 1.0 - level * lax.rsqrt(real * real + imag * imag + 0.25)
                 resid[s, here, :] = (real * factor).astype(BF16)
-                resid[s, window + base : window + base + CHUNK, :] = (imag * factor).astype(BF16)
-        for s in range(PAIR):
-            mid = jnp.dot(inverse[...], resid[s], preferred_element_type=F32).astype(BF16)
-            back_half[s, :, :window] = mid[:window]
-            back_half[s, :, window:] = mid[window:]
-        for s, (row, tile, rest) in enumerate(places):
+                resid[s, window + line : window + line + CHUNK, :] = (imag * factor).astype(BF16)
+                yield
+
+        def rows_back(s):
+            for n in range(2):
+                part = slice(n * window, (n + 1) * window)
+                back_half[s, :, part] = jnp.dot(
+                    inverse[part, :], resid[s], preferred_element_type=F32).astype(BF16)
+                yield
+
+        def columns_back(s):
+            row, tile, rest = places[s]
             back = jnp.dot(back_half[s], forward[...], preferred_element_type=F32)
+            yield
             turn = lax.rem(rest, LANE)
             tail = lane >= rest
-            weight = (group * PAIR + s < total).astype(F32)
-            for base in range(0, window, CHUNK):
-                rows = pl.ds(row + base, CHUNK)
-                here = slice(base, base + CHUNK)
+            weight = (base + s < total).astype(F32)
+            for line in range(0, window, CHUNK):
+                rows = pl.ds(row + line, CHUNK)
+                here = slice(line, line + CHUNK)
                 terms = [[], []]
                 for k in range(2):
                     cols = slice(k * LANE, (k + 1) * LANE)
@@ -164,9 +176,27 @@
                     acc[plane, tile, rows, :] += jnp.where(tail, left, 0.0)
                     acc[plane, tile + 1, rows, :] += jnp.where(tail, right, left)
                     acc[plane, tile + 2, rows, :] += jnp.where(tail, 0.0, right)
+                yield
+
+        for s in range(size):
+            fetch(base + s).wait()
+        stages = (extract, rows_forward, columns_forward, rows_back, columns_back)
+        for step in range(size + len(stages) - 1):
+            running = [
+                stages[step - s](s) for s in reversed(range(size)) if 0 <= step - s < len(stages)]
+            for work in running:
+                for _ in work:
+                    pass
+
+    def full(group, carry):
+        body(group * PAIR, PAIR)
         return carry
 
-    lax.fori_loop(0, groups, body, 0)
+    lax.fori_loop(0, full_groups, full, 0)
+
+    @pl.when(half_group)
+    def _():
+        body(full_groups * PAIR, PAIR // 2)
 
 
 def run_copies(copies):
@@ -420,7 +450,7 @@
             scratch_shapes=make_scratch(window, tiles_held, place, 12),
             compiler_params=params,
             cost_estimate=pl.CostEstimate(
-                flops=32 * window**3 * count, bytes_accessed=8 * 2**20, transcendentals=0),
+                flops=32 * window**3 * count, bytes_accessed=2**20 * count, transcendentals=0),
             name=kernel.__name__,
         )(offsets, slot_counts, amplitude, forward, inverse, illumination, *extra)
 
@@ -433,7 +463,7 @@
     lower = shifted(lower_own, "row", -1)
     bottom_right = shifted(bottom_own, "col", -1)
     part, probe_sum = slots_call(
-        inside_kernel, 8, [(2, tiles, rows, LANE), plane], (object_field,), rows, tiles)
+        inside_kernel, 0, [(2, tiles, rows, LANE), plane], (object_field,), rows, tiles)
     top_right, part = lax.optimization_barrier((top_right, part))
     corner_right = shifted(top_right, "row", -1)
     own, strip, spill, probe_sum = slots_call(

time: 101 us -> 96.3 us (0.953); the launches traced: 102 us -> 96.5 us
  Pallas kernels: 31.2 us -> 22.7 us
  blocking collectives: 36.1 us -> 28.2 us
  waiting for transfers between devices: 9.27 us -> 15.1 us
  starting transfers between devices: 19 us -> 24.7 us
  local copies, waits for them, and re-layouts: 4.82 us -> 2.74 us
  other arithmetic: 0.95 us -> 1.99 us
    pallas_call x3, Pallas kernels: 22.2 us -> 13.7 us  [slots_call(): pl.pallas_call(functools.partial(kernel, shape), out_shape=[sds(*dims) fo...]
    all_to_all x1, blocking collectives: 24.7 us -> 16.3 us  [per_device(): lax.all_to_all(probe_sum.reshape(pieces, -1, window), 'row', 0, 0, tiled=...]
    ppermute x8, waiting for transfers between devices: 6.95 us -> 14.4 us  [shifted(): lax.ppermute(value, axis, [(source, source + steps) for source in range(l...]
    ppermute x8, starting transfers between devices: 14.6 us -> 20.2 us  [shifted(): lax.ppermute(value, axis, [(source, source + steps) for source in range(l...]
    unnamed x19 -> x17, local copies, waits for them, and re-layouts: 4.82 us -> 2.74 us
    ppermute x3, waiting for transfers between devices: 2.32 us -> 0.75 us  [exchange_total(): lax.ppermute(value, axis, [(k, k ^ mask * step) for k in range(count)])]
    add x1, other arithmetic: 0.07 us -> 1.11 us  [per_device(): top_back = shifted(top + corner_back, 'col', 1)]
  transfers between devices with their start and end apart: 11 -> 11, of which waited for: 4 -> 3; matrix products, arithmetic and copies ran while one was open for 1% -> 2% of each run, Pallas kernels for 16% -> 11%
where the time goes in v3:
time: 96.3 us; the launch traced here: 96.5 us
  blocking collectives  28.2 us (29%)
  starting transfers between devices  24.7 us (26%)
  Pallas kernels  22.7 us (24%)
  waiting for transfers between devices  15.1 us (16%)
  local copies, waits for them, and re-layouts  2.74 us (3%)
  other arithmetic  1.99 us (2%)
  between operations  1.04 us (1%)
    ppermute x8, starting transfers between devices, shifted(): lax.ppermute(value, axis, [(source, source + steps) for source in range(l...  20.2 us
    all_to_all x1, blocking collectives, per_device(): lax.all_to_all(probe_sum.reshape(pieces, -1, window), 'row', 0, 0, tiled=...  16.3 us
    ppermute x8, waiting for transfers between devices, shifted(): lax.ppermute(value, axis, [(source, source + steps) for source in range(l...  14.4 us
    pallas_call x3, Pallas kernels, slots_call(): pl.pallas_call(functools.partial(kernel, shape), out_shape=[sds(*dims) fo...  13.7 us
    all_gather x1, blocking collectives, per_device(): summed = lax.all_gather(piece, 'row').reshape(plane)  11.9 us
    pallas_call x2, Pallas kernels, slices(): pl.pallas_call(functools.partial(slice_kernel, spots), out_shape=[jax.Sha...  4.58 us
    pallas_call x2, Pallas kernels, merge(): pl.pallas_call(functools.partial(merge_kernel, places), out_shape=jax.Sha...  4.45 us
    ppermute x3, starting transfers between devices, exchange_total(): lax.ppermute(value, axis, [(k, k ^ mask * step) for k in range(count)])  4.45 us
  transfers between devices with their start and end apart: 11, of which 3 were waited for; matrix products, arithmetic and copies ran while one was open for 2% of the time, Pallas kernels for 11%

profile of v3, /device:TPU:0, one launch (start us, length us, event | category | flops | bytes accessed | tf_op | source)
XLA Modules:
  0.0 96.5 jit_solution(2227157359094704803)
XLA Ops:
  0.6 0.0 copy-start.3
  0.6 0.0 copy-start
  0.7 2.0 %slice_top.1 = f32[2,256,256]{2,1,0:T(8,128)} custom-call(f32[2,512,512]{2,1,0:T(8,128)} %tile_in.8), custom_call_target="tpu_custom_call" | custom-call | tf_op jit(solution)/shard_map/slice_top/pallas_call | solution.py:250
  2.7 2.6 %slice_rest.1 = (f32[2,256,256]{2,1,0:T(8,128)}, f32[2,256,512]{2,1,0:T(8,128)}) custom-call(f32[2,512,512]{2,1,0:T(8,128)} %tile_in.8), custom_call_target="tpu_custom_call" | custom-call | tf_op jit(solution)/shard_map/slice_rest/pallas_call | solution.py:250
  5.3 1.3 %collective-permute-start = (f32[2,256,512]{2,1,0:T(8,128)}, f32[2,256,512]{2,1,0:T(8,128)}, u32[]{:S(2)}, u32[]{:S(2)}) collective-permute-start(f32[2,256,512]{2,1,0:T(8,128)} %get-tuple-element.25), channel_id=1, source_target_pairs={{4,0},{8,4},{12,8},{16,12},{20,16},{24,20},{28,24},{5,1},{9,5},{13... | collective-permute-start | bytes 3145736 | tf_op jit(solution)/shard_map/ppermute | solution.py:23
  6.6 1.3 %collective-permute-start.1 = (f32[2,256,256]{2,1,0:T(8,128)}, f32[2,256,256]{2,1,0:T(8,128)}, u32[]{:S(2)}, u32[]{:S(2)}) collective-permute-start(f32[2,256,256]{2,1,0:T(8,128)} %slice_top.1), channel_id=1, source_target_pairs={{1,0},{2,1},{3,2},{5,4},{6,5},{7,6},{9,8},{10,9},{11,10},{13,12},{... | collective-permute-start | bytes 1572872 | tf_op jit(solution)/shard_map/ppermute | solution.py:23
  7.9 1.3 %collective-permute-start.2 = (f32[2,256,256]{2,1,0:T(8,128)}, f32[2,256,256]{2,1,0:T(8,128)}, u32[]{:S(2)}, u32[]{:S(2)}) collective-permute-start(f32[2,256,256]{2,1,0:T(8,128)} %get-tuple-element.29), channel_id=1, source_target_pairs={{1,0},{2,1},{3,2},{5,4},{6,5},{7,6},{9,8},{10,9},{11,10},{13,12},{... | collective-permute-start | bytes 1572872 | tf_op jit(solution)/shard_map/ppermute | solution.py:23
  9.2 0.1 copy.15.offs
  9.3 0.0 copy-start.1
  9.3 1.6 %copy-done.1 = bf16[16,256,256]{2,1,0:T(8,128)(2,1)S(1)} copy-done((bf16[16,256,256]{2,1,0:T(8,128)(2,1)S(1)}, bf16[16,256,256]{2,1,0:T(8,128)(2,1)}, u32[]{:S(2)}) %copy-start.1) | copy-done | bytes 2097176
  10.9 1.0 %copy-done.4 = bf16[512,512]{1,0:T(8,128)(2,1)S(1)} copy-done((bf16[512,512]{1,0:T(8,128)(2,1)S(1)}, bf16[512,512]{1,0:T(8,128)(2,1)}, u32[]{:S(2)}) %copy-start.4) | copy-done | bytes 524312
  11.9 4.3 %inside_kernel.1 = (f32[2,4,512,128]{3,2,1,0:T(8,128)S(1)}, f32[2,256,256]{2,1,0:T(8,128)S(1)}) custom-call(s32[16,2]{1,0:T(8,128)S(1)} %copy.15.offs, s32[32]{0:T(128)S(1)} %copy-done.6, bf16[16,256,256]{2,1,0:T(8,128)(2,1)S(1)} %copy-done.1, bf16[512,512]{1,0:T(8,128)(2,1)S(1)} %copy-done.4, bf16[512,512]{1,0:T(8,128)(2,1)S(1)} %copy-done.3, ...), custom_call_target="tpu_custom_call" | custom-call | tf_op jit(solution)/shard_map/inside_kernel/pallas_call | solution.py:444
  16.2 8.0 %collective-permute-done.1.top_in = f32[2,256,256]{2,1,0:T(8,128)} collective-permute-done((f32[2,256,256]{2,1,0:T(8,128)}, f32[2,256,256]{2,1,0:T(8,128)}, u32[]{:S(2)}, u32[]{:S(2)}) %collective-permute-start.1) | collective-permute-done | bytes 524320 | tf_op jit(solution)/shard_map/ppermute | solution.py:23
  24.2 1.3 %collective-permute-start.3 = (f32[2,256,256]{2,1,0:T(8,128)}, f32[2,256,256]{2,1,0:T(8,128)S(1)}, u32[]{:S(2)}, u32[]{:S(2)}) collective-permute-start(f32[2,256,256]{2,1,0:T(8,128)} %collective-permute-done.1.top_in), channel_id=1, source_target_pairs={{4,0},{8,4},{12,8},{16,12},{20,16},{24,20},{28,24},{5,1},{9,5},{13... | collective-permute-start | bytes 1572872 | tf_op jit(solution)/shard_map/ppermute | solution.py:23
  25.5 3.5 %below_kernel.1 = (f32[2,512,512]{2,1,0:T(8,128)}, f32[2,256,512]{2,1,0:T(8,128)}, f32[2,2,768,128]{3,2,1,0:T(8,128)S(1)}, f32[2,256,256]{2,1,0:T(8,128)S(1)}) custom-call(s32[16,2]{1,0:T(8,128)S(1)} %copy.15.offs, s32[32]{0:T(128)S(1)} %copy-done.6, bf16[16,256,256]{2,1,0:T(8,128)(2,1)S(1)} %copy-done.1, bf16[512,512]{1,0:T(8,128)(2,1)S(1)} %copy-done.4, ...), custom_call_target="tpu_custom_call" | custom-call | flops 4294967296 | bytes 8388608 | tf_op jit(solution)/shard_map/below_kernel/pallas_call | solution.py:444
  29.1 6.4 %collective-permute-done.2.bottom_in = f32[2,256,256]{2,1,0:T(8,128)} collective-permute-done((f32[2,256,256]{2,1,0:T(8,128)}, f32[2,256,256]{2,1,0:T(8,128)}, u32[]{:S(2)}, u32[]{:S(2)}) %collective-permute-start.2) | collective-permute-done | bytes 524320 | tf_op jit(solution)/shard_map/ppermute | solution.py:23
  35.5 5.8 %across_kernel.1 = (f32[2,512,512]{2,1,0:T(8,128)}, f32[2,256,512]{2,1,0:T(8,128)}, f32[2,256,256]{2,1,0:T(8,128)S(1)}, f32[2,256,256]{2,1,0:T(8,128)S(1)}, f32[...) custom-call(s32[16,2]{1,0:T(8,128)S(1)} %copy.15.offs, ...), custom_call_target="tpu_custom_call", output_to_operand_aliasing={{0}: (13, {}), {1}: (14, {})} | custom-call | flops 4294967296 | bytes 8388608 | tf_op jit(solution)/shard_map/across_kernel/pallas_call | solution.py:444
  41.3 0.0 copy-start.5
  41.3 8.2 %collective-permute-start.4 = (f32[2,256,256]{2,1,0:T(8,128)S(1)}, f32[2,256,256]{2,1,0:T(8,128)S(1)}, u32[]{:S(2)}, u32[]{:S(2)}) collective-permute-start(f32[2,256,256]{2,1,0:T(8,128)S(1)} %get-tuple-element.38), channel_id=1, source_target_pairs={{0,4},{4,8},{8,12},{12,16},{16,20},{20,24},{24,28},{1,5},{5,9},{9,... | collective-permute-start | bytes 1572872 | tf_op jit(solution)/shard_map/ppermute | solution.py:23
  49.6 3.5 %collective-permute-start.5 = (f32[2,256,256]{2,1,0:T(8,128)S(1)}, f32[2,256,256]{2,1,0:T(8,128)S(1)}, u32[]{:S(2)}, u32[]{:S(2)}) collective-permute-start(f32[2,256,256]{2,1,0:T(8,128)S(1)} %get-tuple-element.39), channel_id=1, source_target_pairs={{0,1},{1,2},{2,3},{4,5},{5,6},{6,7},{8,9},{9,10},{10,11},{12,13},{... | collective-permute-start | bytes 1572872 | tf_op jit(solution)/shard_map/ppermute | solution.py:23
  53.1 16.3 %all_to_all.5 = f32[8,64,256]{2,1,0:T(8,128)S(1)} all-to-all(f32[8,64,256]{2,1,0:T(8,128)S(1)} %bitcast.2), channel_id=1, replica_groups=mesh['row'=8,'col'=4] {'row'}, dimensions={0} | all-to-all | bytes 1048576 | tf_op jit(solution)/shard_map/all_to_all | solution.py:481
  69.4 1.4 %collective-permute-start.6 = (f32[2,256,512]{2,1,0:T(8,128)}, f32[2,256,512]{2,1,0:T(8,128)S(1)}, u32[]{:S(2)}, u32[]{:S(2)}) collective-permute-start(f32[2,256,512]{2,1,0:T(8,128)} %get-tuple-element.41), channel_id=1, source_target_pairs={{0,4},{4,8},{8,12},{12,16},{16,20},{20,24},{24,28},{1,5},{5,9},{9,... | collective-permute-start | bytes 3145736 | tf_op jit(solution)/shard_map/ppermute | solution.py:23
  70.8 0.1 collective-permute-start.10
  70.9 1.8 %collective-permute-start.9 = (f32[64,256]{1,0:T(8,128)S(1)}, f32[64,256]{1,0:T(8,128)S(1)}, u32[]{:S(2)}, u32[]{:S(2)}) collective-permute-start(f32[64,256]{1,0:T(8,128)S(1)} %reduce_sum.9), channel_id=1, source_target_pairs={{0,2},{1,3},{2,0},{3,1},{4,6},{5,7},{6,4},{7,5},{8,10},{9,11},{10,... | collective-permute-start | bytes 196616 | tf_op jit(solution)/shard_map/ppermute | solution.py:419
  72.7 2.6 %collective-permute-start.8 = (f32[64,256]{1,0:T(8,128)S(1)}, f32[64,256]{1,0:T(8,128)S(1)}, u32[]{:S(2)}, u32[]{:S(2)}) collective-permute-start(f32[64,256]{1,0:T(8,128)S(1)} %reduce_sum.9), channel_id=1, source_target_pairs={{0,1},{1,0},{2,3},{3,2},{4,5},{5,4},{6,7},{7,6},{8,9},{9,8},{10,11... | collective-permute-start | bytes 196616 | tf_op jit(solution)/shard_map/ppermute | solution.py:419
  75.3 1.1 %add.12 = f32[2,256,256]{2,1,0:T(8,128)S(1)} add(f32[2,256,256]{2,1,0:T(8,128)} %copy-done.5, f32[2,256,256]{2,1,0:T(8,128)S(1)} %collective-permute-done.4) | non-fusion elementwise | flops 131072 | bytes 1572864 | tf_op jit(solution)/shard_map/add | solution.py:485
  76.4 1.9 %collective-permute-start.7 = (f32[2,256,256]{2,1,0:T(8,128)S(1)}, f32[2,256,256]{2,1,0:T(8,128)S(1)}, u32[]{:S(2)}, u32[]{:S(2)}) collective-permute-start(f32[2,256,256]{2,1,0:T(8,128)S(1)} %add.12), channel_id=1, source_target_pairs={{0,1},{1,2},{2,3},{4,5},{5,6},{6,7},{8,9},{9,10},{10,11},{12,13},{... | collective-permute-start | bytes 1572872 | tf_op jit(solution)/shard_map/ppermute | solution.py:23
  78.4 0.7 collective-permute-done.8
  79.1 11.9 %all-gather = f32[512,256]{1,0:T(8,128)S(1)} all-gather(f32[64,256]{1,0:T(8,128)S(1)} %add_add_fusion), channel_id=2, replica_groups=mesh['row'=8,'col'=4] {'row'}, dimensions={0}, use_global_device_ids=true | all-gather | bytes 589824 | tf_op jit(solution)/shard_map/all_gather | solution.py:488
  91.0 0.8 broadcast_multiply_fusion
  91.8 2.5 %first_merge.1.own_in = f32[2,512,512]{2,1,0:T(8,128)} custom-call(f32[2,512,512]{2,1,0:T(8,128)} %get-tuple-element.36.own_in, f32[2,256,512]{2,1,0:T(8,128)S(1)} %collective-permute-done.6.refs_0_, f32[2,256,256]{2,1,0:T(8,128)S(1)} %collective-permute-done.5.refs_1_), custom_call_target="tpu_custom_call", output_to_operand_aliasing={{}: (0, {})} | custom-call | tf_op jit(solution)/shard_map/first_merge/pallas_call | solution.py:285
  94.4 1.9 %last_merge.1 = f32[2,512,512]{2,1,0:T(8,128)} custom-call(f32[2,512,512]{2,1,0:T(8,128)} %first_merge.1.own_in, f32[2,256,256]{2,1,0:T(8,128)S(1)} %collective-permute-done.7.refs_0_), custom_call_target="tpu_custom_call", output_to_operand_aliasing={{}: (0, {})} | custom-call | tf_op jit(solution)/shard_map/last_merge/pallas_call | solution.py:285
  (20 shorter events, 0.1 us)
Async XLA Ops:
  0.6 8.6 %copy-start.3 = (bf16[512,512]{1,0:T(8,128)(2,1)S(1)}, bf16[512,512]{1,0:T(8,128)(2,1)}, u32[]{:S(2)}) copy-start(bf16[512,512]{1,0:T(8,128)(2,1)} %constant.9.clone.inverse) | copy-start | bytes 1572868
  0.6 8.6 %copy-start = (f32[2,512,512]{2,1,0:T(8,128)S(1)}, f32[2,512,512]{2,1,0:T(8,128)}, u32[]{:S(2)}) copy-start(f32[2,512,512]{2,1,0:T(8,128)} %tile_in.8) | copy-start | bytes 6291460
  0.7 8.5 %copy-start.7 = (s32[16,2]{0,1:T(2,128)S(1)}, s32[16,2]{0,1:T(2,128)}, u32[]{:S(2)}) copy-start(s32[16,2]{0,1:T(2,128)} %param.10) | copy-start | bytes 388
  0.7 8.6 %copy-start.6 = (s32[32]{0:T(128)S(1)}, s32[32]{0:T(128)}, u32[]{:S(2)}) copy-start(s32[32]{0:T(128)} %counts.5) | copy-start | bytes 388
  0.7 8.6 %copy-start.2 = (f32[2,256,256]{2,1,0:T(8,128)S(1)}, f32[2,256,256]{2,1,0:T(8,128)}, u32[]{:S(2)}) copy-start(f32[2,256,256]{2,1,0:T(8,128)} %probe.5) | copy-start | bytes 1572868
  5.3 20.3 %collective-permute-start = (f32[2,256,512]{2,1,0:T(8,128)}, f32[2,256,512]{2,1,0:T(8,128)}, u32[]{:S(2)}, u32[]{:S(2)}) collective-permute-start(f32[2,256,512]{2,1,0:T(8,128)} %get-tuple-element.25), channel_id=1, source_target_pairs={{4,0},{8,4},{12,8},{16,12},{20,16},{24,20},{28,24},{5,1},{9,5},{13... | collective-permute-start | bytes 3145736 | tf_op jit(solution)/shard_map/ppermute | solution.py:23
  6.6 17.7 %collective-permute-start.1 = (f32[2,256,256]{2,1,0:T(8,128)}, f32[2,256,256]{2,1,0:T(8,128)}, u32[]{:S(2)}, u32[]{:S(2)}) collective-permute-start(f32[2,256,256]{2,1,0:T(8,128)} %slice_top.1), channel_id=1, source_target_pairs={{1,0},{2,1},{3,2},{5,4},{6,5},{7,6},{9,8},{10,9},{11,10},{13,12},{... | collective-permute-start | bytes 1572872 | tf_op jit(solution)/shard_map/ppermute | solution.py:23
  7.9 27.6 %collective-permute-start.2 = (f32[2,256,256]{2,1,0:T(8,128)}, f32[2,256,256]{2,1,0:T(8,128)}, u32[]{:S(2)}, u32[]{:S(2)}) collective-permute-start(f32[2,256,256]{2,1,0:T(8,128)} %get-tuple-element.29), channel_id=1, source_target_pairs={{1,0},{2,1},{3,2},{5,4},{6,5},{7,6},{9,8},{10,9},{11,10},{13,12},{... | collective-permute-start | bytes 1572872 | tf_op jit(solution)/shard_map/ppermute | solution.py:23
  9.3 1.6 %copy-start.1 = (bf16[16,256,256]{2,1,0:T(8,128)(2,1)S(1)}, bf16[16,256,256]{2,1,0:T(8,128)(2,1)}, u32[]{:S(2)}) copy-start(bf16[16,256,256]{2,1,0:T(8,128)(2,1)} %amplitude.5) | copy-start | bytes 6291460
  10.9 1.0 %copy-start.4 = (bf16[512,512]{1,0:T(8,128)(2,1)S(1)}, bf16[512,512]{1,0:T(8,128)(2,1)}, u32[]{:S(2)}) copy-start(bf16[512,512]{1,0:T(8,128)(2,1)} %constant.8.clone.forward) | copy-start | bytes 1572868
  24.2 11.2 %collective-permute-start.3 = (f32[2,256,256]{2,1,0:T(8,128)}, f32[2,256,256]{2,1,0:T(8,128)S(1)}, u32[]{:S(2)}, u32[]{:S(2)}) collective-permute-start(f32[2,256,256]{2,1,0:T(8,128)} %collective-permute-done.1.top_in), channel_id=1, source_target_pairs={{4,0},{8,4},{12,8},{16,12},{20,16},{24,20},{28,24},{5,1},{9,5},{13... | collective-permute-start | bytes 1572872 | tf_op jit(solution)/shard_map/ppermute | solution.py:23
  41.3 28.1 %copy-start.5 = (f32[2,256,256]{2,1,0:T(8,128)}, f32[2,256,256]{2,1,0:T(8,128)S(1)}, u32[]{:S(2)}) copy-start(f32[2,256,256]{2,1,0:T(8,128)S(1)} %get-tuple-element.43) | copy-start | bytes 1572868
  41.3 28.1 %collective-permute-start.4 = (f32[2,256,256]{2,1,0:T(8,128)S(1)}, f32[2,256,256]{2,1,0:T(8,128)S(1)}, u32[]{:S(2)}, u32[]{:S(2)}) collective-permute-start(f32[2,256,256]{2,1,0:T(8,128)S(1)} %get-tuple-element.38), channel_id=1, source_target_pairs={{0,4},{4,8},{8,12},{12,16},{16,20},{20,24},{24,28},{1,5},{5,9},{9,... | collective-permute-start | bytes 1572872 | tf_op jit(solution)/shard_map/ppermute | solution.py:23
  49.6 19.8 %collective-permute-start.5 = (f32[2,256,256]{2,1,0:T(8,128)S(1)}, f32[2,256,256]{2,1,0:T(8,128)S(1)}, u32[]{:S(2)}, u32[]{:S(2)}) collective-permute-start(f32[2,256,256]{2,1,0:T(8,128)S(1)} %get-tuple-element.39), channel_id=1, source_target_pairs={{0,1},{1,2},{2,3},{4,5},{5,6},{6,7},{8,9},{9,10},{10,11},{12,13},{... | collective-permute-start | bytes 1572872 | tf_op jit(solution)/shard_map/ppermute | solution.py:23
  69.4 22.4 %collective-permute-start.6 = (f32[2,256,512]{2,1,0:T(8,128)}, f32[2,256,512]{2,1,0:T(8,128)S(1)}, u32[]{:S(2)}, u32[]{:S(2)}) collective-permute-start(f32[2,256,512]{2,1,0:T(8,128)} %get-tuple-element.41), channel_id=1, source_target_pairs={{0,4},{4,8},{8,12},{12,16},{16,20},{20,24},{24,28},{1,5},{5,9},{9,... | collective-permute-start | bytes 3145736 | tf_op jit(solution)/shard_map/ppermute | solution.py:23
  70.8 7.5 %collective-permute-start.10 = (f32[64,256]{1,0:T(8,128)S(1)}, f32[64,256]{1,0:T(8,128)S(1)}, u32[]{:S(2)}, u32[]{:S(2)}) collective-permute-start(f32[64,256]{1,0:T(8,128)S(1)} %reduce_sum.9), channel_id=1, source_target_pairs={{0,3},{1,2},{2,1},{3,0},{4,7},{5,6},{6,5},{7,4},{8,11},{9,10},{10,... | collective-permute-start | bytes 196616 | tf_op jit(solution)/shard_map/ppermute | solution.py:419
  70.9 7.4 %collective-permute-start.9 = (f32[64,256]{1,0:T(8,128)S(1)}, f32[64,256]{1,0:T(8,128)S(1)}, u32[]{:S(2)}, u32[]{:S(2)}) collective-permute-start(f32[64,256]{1,0:T(8,128)S(1)} %reduce_sum.9), channel_id=1, source_target_pairs={{0,2},{1,3},{2,0},{3,1},{4,6},{5,7},{6,4},{7,5},{8,10},{9,11},{10,... | collective-permute-start | bytes 196616 | tf_op jit(solution)/shard_map/ppermute | solution.py:419
  72.7 6.4 %collective-permute-start.8 = (f32[64,256]{1,0:T(8,128)S(1)}, f32[64,256]{1,0:T(8,128)S(1)}, u32[]{:S(2)}, u32[]{:S(2)}) collective-permute-start(f32[64,256]{1,0:T(8,128)S(1)} %reduce_sum.9), channel_id=1, source_target_pairs={{0,1},{1,0},{2,3},{3,2},{4,5},{5,4},{6,7},{7,6},{8,9},{9,8},{10,11... | collective-permute-start | bytes 196616 | tf_op jit(solution)/shard_map/ppermute | solution.py:419
  76.4 18.0 %collective-permute-start.7 = (f32[2,256,256]{2,1,0:T(8,128)S(1)}, f32[2,256,256]{2,1,0:T(8,128)S(1)}, u32[]{:S(2)}, u32[]{:S(2)}) collective-permute-start(f32[2,256,256]{2,1,0:T(8,128)S(1)} %add.12), channel_id=1, source_target_pairs={{0,1},{1,2},{2,3},{4,5},{5,6},{6,7},{8,9},{9,10},{10,11},{12,13},{... | collective-permute-start | bytes 1572872 | tf_op jit(solution)/shard_map/ppermute | solution.py:23

commit v4 on v3

--- a/solution.py
+++ b/solution.py
@@ -12,7 +12,7 @@
 LANE = 128
 CHUNK = 32
 PAIR = 4
-VMEM_LIMIT = 28 * 1024 * 1024
+VMEM_LIMIT = 44 * 1024 * 1024
 F32 = jnp.float32
 BF16 = jnp.bfloat16
 
@@ -163,7 +163,7 @@
                     cols = slice(k * LANE, (k + 1) * LANE)
                     real = back[here, k * LANE : (k + 1) * LANE]
                     imag = back[here, window + k * LANE : window + (k + 1) * LANE]
-                    if s:
+                    if s == size - 1:
                         real, imag = real * weight, imag * weight
                     probe_real, probe_imag = probe[0, here, cols], probe[1, here, cols]
                     patch_real, patch_imag = patch[s, 0, here, cols], patch[s, 1, here, cols]
@@ -455,10 +455,10 @@
         )(offsets, slot_counts, amplitude, forward, inverse, illumination, *extra)
 
     plane = (2, window, window)
-    (top_own,) = slices(object_field, ((0, window, 0, window),), "slice_top")
-    tile, top_own = lax.optimization_barrier((object_field, top_own))
-    bottom_own, lower_own = slices(
-        tile, ((window, rows - window, 0, window), (0, window, 0, cols)), "slice_rest")
+    top_own, bottom_own, lower_own = slices(
+        object_field,
+        ((0, window, 0, window), (window, rows - window, 0, window), (0, window, 0, cols)),
+        "slice_tile")
     top_right = shifted(top_own, "col", -1)
     lower = shifted(lower_own, "row", -1)
     bottom_right = shifted(bottom_own, "col", -1)

time: 96.3 us -> 95.6 us (level)
  waiting for transfers between devices: 15.1 us -> 7.98 us
  Pallas kernels: 22.7 us -> 29.6 us
  local copies, waits for them, and re-layouts: 2.74 us -> 6.16 us
  starting transfers between devices: 24.7 us -> 21.5 us
  other arithmetic: 1.99 us -> 0.95 us
    pallas_call x3, Pallas kernels: 13.7 us -> 22.1 us  [slots_call(): pl.pallas_call(functools.partial(kernel, shape), out_shape=[sds(*dims) fo...]
    ppermute x8, waiting for transfers between devices: 14.4 us -> 6.25 us  [shifted(): lax.ppermute(value, axis, [(source, source + steps) for source in range(l...]
    ppermute x8, starting transfers between devices: 20.2 us -> 14.1 us  [shifted(): lax.ppermute(value, axis, [(source, source + steps) for source in range(l...]
    unnamed x17 -> x25, local copies, waits for them, and re-layouts: 2.74 us -> 6.16 us
    ppermute x3, starting transfers between devices: 4.45 us -> 7.42 us  [exchange_total(): lax.ppermute(value, axis, [(k, k ^ mask * step) for k in range(count)])]
    all_to_all x1, blocking collectives: 16.3 us -> 18 us  [per_device(): lax.all_to_all(probe_sum.reshape(pieces, -1, window), 'row', 0, 0, tiled=...]
    pallas_call x2 -> x1, Pallas kernels: 4.58 us -> 3.04 us  [slices(): pl.pallas_call(functools.partial(slice_kernel, spots), out_shape=[jax.Sha...]
    all_gather x1, blocking collectives: 11.9 us -> 10.8 us  [per_device(): summed = lax.all_gather(piece, 'row').reshape(plane)]
  transfers between devices with their start and end apart: 11 -> 11, of which waited for: 3 -> 4; matrix products, arithmetic and copies ran while one was open for 2% -> 1% of each run, Pallas kernels for 11% -> 16%
where the time goes in v4:
time: 95.6 us; the launch traced here: 96 us
  Pallas kernels  29.6 us (31%)
  blocking collectives  28.8 us (30%)
  starting transfers between devices  21.5 us (22%)
  waiting for transfers between devices  7.98 us (8%)
  local copies, waits for them, and re-layouts  6.16 us (6%)
  between operations  1.01 us (1%)
    pallas_call x3, Pallas kernels, slots_call(): pl.pallas_call(functools.partial(kernel, shape), out_shape=[sds(*dims) fo...  22.1 us
    all_to_all x1, blocking collectives, per_device(): lax.all_to_all(probe_sum.reshape(pieces, -1, window), 'row', 0, 0, tiled=...  18 us
    ppermute x8, starting transfers between devices, shifted(): lax.ppermute(value, axis, [(source, source + steps) for source in range(l...  14.1 us
    all_gather x1, blocking collectives, per_device(): summed = lax.all_gather(piece, 'row').reshape(plane)  10.8 us
    ppermute x3, starting transfers between devices, exchange_total(): lax.ppermute(value, axis, [(k, k ^ mask * step) for k in range(count)])  7.42 us
    ppermute x8, waiting for transfers between devices, shifted(): lax.ppermute(value, axis, [(source, source + steps) for source in range(l...  6.25 us
    unnamed x25, local copies, waits for them, and re-layouts  6.16 us
    pallas_call x2, Pallas kernels, merge(): pl.pallas_call(functools.partial(merge_kernel, places), out_shape=jax.Sha...  4.45 us
  transfers between devices with their start and end apart: 11, of which 4 were waited for; matrix products, arithmetic and copies ran while one was open for 1% of the time, Pallas kernels for 16%

profile of v4, /device:TPU:0, one launch (start us, length us, event | category | flops | bytes accessed | tf_op | source)
XLA Modules:
  0.0 96.0 jit_solution(1685904280771243559)
XLA Ops:
  0.6 0.0 copy-start
  0.7 3.0 %slice_tile.1 = (f32[2,256,256]{2,1,0:T(8,128)}, f32[2,256,256]{2,1,0:T(8,128)}, f32[2,256,512]{2,1,0:T(8,128)}) custom-call(f32[2,512,512]{2,1,0:T(8,128)} %tile_in.7), custom_call_target="tpu_custom_call" | custom-call | tf_op jit(solution)/shard_map/slice_tile/pallas_call | solution.py:250
  3.7 1.3 %collective-permute-start = (f32[2,256,512]{2,1,0:T(8,128)}, f32[2,256,512]{2,1,0:T(8,128)S(1)}, u32[]{:S(2)}, u32[]{:S(2)}) collective-permute-start(f32[2,256,512]{2,1,0:T(8,128)} %get-tuple-element.23), channel_id=1, source_target_pairs={{4,0},{8,4},{12,8},{16,12},{20,16},{24,20},{28,24},{5,1},{9,5},{13... | collective-permute-start | bytes 3145736 | tf_op jit(solution)/shard_map/ppermute | solution.py:23
  5.0 1.3 %collective-permute-start.1 = (f32[2,256,256]{2,1,0:T(8,128)}, f32[2,256,256]{2,1,0:T(8,128)}, u32[]{:S(2)}, u32[]{:S(2)}) collective-permute-start(f32[2,256,256]{2,1,0:T(8,128)} %get-tuple-element.24), channel_id=1, source_target_pairs={{1,0},{2,1},{3,2},{5,4},{6,5},{7,6},{9,8},{10,9},{11,10},{13,12},{... | collective-permute-start | bytes 1572872 | tf_op jit(solution)/shard_map/ppermute | solution.py:23
  6.3 1.3 %collective-permute-start.2 = (f32[2,256,256]{2,1,0:T(8,128)}, f32[2,256,256]{2,1,0:T(8,128)}, u32[]{:S(2)}, u32[]{:S(2)}) collective-permute-start(f32[2,256,256]{2,1,0:T(8,128)} %get-tuple-element.27), channel_id=1, source_target_pairs={{1,0},{2,1},{3,2},{5,4},{6,5},{7,6},{9,8},{10,9},{11,10},{13,12},{... | collective-permute-start | bytes 1572872 | tf_op jit(solution)/shard_map/ppermute | solution.py:23
  7.6 0.1 copy.15.offs
  7.7 1.6 %copy-done.1 = bf16[16,256,256]{2,1,0:T(8,128)(2,1)S(1)} copy-done((bf16[16,256,256]{2,1,0:T(8,128)(2,1)S(1)}, bf16[16,256,256]{2,1,0:T(8,128)(2,1)}, u32[]{:S(2)}) %copy-start.1) | copy-done | bytes 2097176
  9.3 1.0 %copy-done.3 = f32[2,256,256]{2,1,0:T(8,128)S(1)} copy-done((f32[2,256,256]{2,1,0:T(8,128)S(1)}, f32[2,256,256]{2,1,0:T(8,128)}, u32[]{:S(2)}) %copy-start.3) | copy-done | bytes 524312
  10.3 1.0 %copy-done.5 = bf16[512,512]{1,0:T(8,128)(2,1)S(1)} copy-done((bf16[512,512]{1,0:T(8,128)(2,1)S(1)}, bf16[512,512]{1,0:T(8,128)(2,1)}, u32[]{:S(2)}) %copy-start.5) | copy-done | bytes 524312
  11.4 1.0 %copy-done.7 = bf16[512,512]{1,0:T(8,128)(2,1)S(1)} copy-done((bf16[512,512]{1,0:T(8,128)(2,1)S(1)}, bf16[512,512]{1,0:T(8,128)(2,1)}, u32[]{:S(2)}) %copy-start.7) | copy-done | bytes 524312
  12.4 6.0 %inside_kernel.1 = (f32[2,4,512,128]{3,2,1,0:T(8,128)S(1)}, f32[2,256,256]{2,1,0:T(8,128)S(1)}) custom-call(s32[16,2]{1,0:T(8,128)S(1)} %copy.15.offs, s32[32]{0:T(128)S(1)} %copy-done.9, bf16[16,256,256]{2,1,0:T(8,128)(2,1)S(1)} %copy-done.1, bf16[512,512]{1,0:T(8,128)(2,1)S(1)} %copy-done.7, bf16[512,512]{1,0:T(8,128)(2,1)S(1)} %copy-done.5, ...), custom_call_target="tpu_custom_call" | custom-call | tf_op jit(solution)/shard_map/inside_kernel/pallas_call | solution.py:444
  18.5 1.3 %copy-done.10 = f32[2,4,512,128]{3,2,1,0:T(8,128)} copy-done((f32[2,4,512,128]{3,2,1,0:T(8,128)}, f32[2,4,512,128]{3,2,1,0:T(8,128)S(1)}, u32[]{:S(2)}) %copy-start.10) | copy-done | bytes 2097176
  19.8 2.9 %collective-permute-done.1.top_in = f32[2,256,256]{2,1,0:T(8,128)} collective-permute-done((f32[2,256,256]{2,1,0:T(8,128)}, f32[2,256,256]{2,1,0:T(8,128)}, u32[]{:S(2)}, u32[]{:S(2)}) %collective-permute-start.1) | collective-permute-done | bytes 524320 | tf_op jit(solution)/shard_map/ppermute | solution.py:23
  22.7 1.3 %collective-permute-start.3 = (f32[2,256,256]{2,1,0:T(8,128)}, f32[2,256,256]{2,1,0:T(8,128)S(1)}, u32[]{:S(2)}, u32[]{:S(2)}) collective-permute-start(f32[2,256,256]{2,1,0:T(8,128)} %collective-permute-done.1.top_in), channel_id=1, source_target_pairs={{4,0},{8,4},{12,8},{16,12},{20,16},{24,20},{28,24},{5,1},{9,5},{13... | collective-permute-start | bytes 1572872 | tf_op jit(solution)/shard_map/ppermute | solution.py:23
  24.0 6.5 %below_kernel.1 = (f32[2,512,512]{2,1,0:T(8,128)}, f32[2,256,512]{2,1,0:T(8,128)}, f32[2,2,768,128]{3,2,1,0:T(8,128)S(1)}, f32[2,256,256]{2,1,0:T(8,128)S(1)}) custom-call(s32[16,2]{1,0:T(8,128)S(1)} %copy.15.offs, s32[32]{0:T(128)S(1)} %copy-done.9, bf16[16,256,256]{2,1,0:T(8,128)(2,1)S(1)} %copy-done.2, bf16[512,512]{1,0:T(8,128)(2,1)S(1)} %copy-done.7, ...), custom_call_target="tpu_custom_call" | custom-call | flops 4294967296 | bytes 8388608 | tf_op jit(solution)/shard_map/below_kernel/pallas_call | solution.py:444
  30.5 3.4 %collective-permute-done.2.bottom_in = f32[2,256,256]{2,1,0:T(8,128)} collective-permute-done((f32[2,256,256]{2,1,0:T(8,128)}, f32[2,256,256]{2,1,0:T(8,128)}, u32[]{:S(2)}, u32[]{:S(2)}) %collective-permute-start.2) | collective-permute-done | bytes 524320 | tf_op jit(solution)/shard_map/ppermute | solution.py:23
  33.9 9.6 %across_kernel.1 = (f32[2,512,512]{2,1,0:T(8,128)}, f32[2,256,512]{2,1,0:T(8,128)}, f32[2,256,256]{2,1,0:T(8,128)S(1)}, f32[2,256,256]{2,1,0:T(8,128)S(1)}, f32[...) custom-call(s32[16,2]{1,0:T(8,128)S(1)} %copy.15.offs, ...), custom_call_target="tpu_custom_call", output_to_operand_aliasing={{0}: (13, {}), {1}: (14, {})} | custom-call | flops 4294967296 | bytes 8388608 | tf_op jit(solution)/shard_map/across_kernel/pallas_call | solution.py:444
  43.5 1.3 %collective-permute-start.4 = (f32[2,256,256]{2,1,0:T(8,128)S(1)}, f32[2,256,256]{2,1,0:T(8,128)S(1)}, u32[]{:S(2)}, u32[]{:S(2)}) collective-permute-start(f32[2,256,256]{2,1,0:T(8,128)S(1)} %get-tuple-element.36), channel_id=1, source_target_pairs={{0,4},{4,8},{8,12},{12,16},{16,20},{20,24},{24,28},{1,5},{5,9},{9,... | collective-permute-start | bytes 1572872 | tf_op jit(solution)/shard_map/ppermute | solution.py:23
  44.9 2.8 %collective-permute-start.5 = (f32[2,256,256]{2,1,0:T(8,128)S(1)}, f32[2,256,256]{2,1,0:T(8,128)S(1)}, u32[]{:S(2)}, u32[]{:S(2)}) collective-permute-start(f32[2,256,256]{2,1,0:T(8,128)S(1)} %get-tuple-element.37), channel_id=1, source_target_pairs={{0,1},{1,2},{2,3},{4,5},{5,6},{6,7},{8,9},{9,10},{10,11},{12,13},{... | collective-permute-start | bytes 1572872 | tf_op jit(solution)/shard_map/ppermute | solution.py:23
  47.6 18.0 %all_to_all.5 = f32[8,64,256]{2,1,0:T(8,128)S(1)} all-to-all(f32[8,64,256]{2,1,0:T(8,128)S(1)} %bitcast.2), channel_id=1, replica_groups=mesh['row'=8,'col'=4] {'row'}, dimensions={0} | all-to-all | bytes 1048576 | tf_op jit(solution)/shard_map/all_to_all | solution.py:481
  65.6 1.3 %collective-permute-start.6 = (f32[2,256,512]{2,1,0:T(8,128)}, f32[2,256,512]{2,1,0:T(8,128)S(1)}, u32[]{:S(2)}, u32[]{:S(2)}) collective-permute-start(f32[2,256,512]{2,1,0:T(8,128)} %get-tuple-element.39), channel_id=1, source_target_pairs={{0,4},{4,8},{8,12},{12,16},{16,20},{20,24},{24,28},{1,5},{5,9},{9,... | collective-permute-start | bytes 3145736 | tf_op jit(solution)/shard_map/ppermute | solution.py:23
  67.0 5.9 %collective-permute-start.10 = (f32[64,256]{1,0:T(8,128)S(1)}, f32[64,256]{1,0:T(8,128)S(1)}, u32[]{:S(2)}, u32[]{:S(2)}) collective-permute-start(f32[64,256]{1,0:T(8,128)S(1)} %reduce_sum.9), channel_id=1, source_target_pairs={{0,3},{1,2},{2,1},{3,0},{4,7},{5,6},{6,5},{7,4},{8,11},{9,10},{10,... | collective-permute-start | bytes 196616 | tf_op jit(solution)/shard_map/ppermute | solution.py:419
  73.0 1.0 %collective-permute-start.9 = (f32[64,256]{1,0:T(8,128)S(1)}, f32[64,256]{1,0:T(8,128)S(1)}, u32[]{:S(2)}, u32[]{:S(2)}) collective-permute-start(f32[64,256]{1,0:T(8,128)S(1)} %reduce_sum.9), channel_id=1, source_target_pairs={{0,2},{1,3},{2,0},{3,1},{4,6},{5,7},{6,4},{7,5},{8,10},{9,11},{10,... | collective-permute-start | bytes 196616 | tf_op jit(solution)/shard_map/ppermute | solution.py:419
  74.0 0.5 collective-permute-start.8
  74.5 0.1 add.12
  74.5 3.5 %collective-permute-start.7 = (f32[2,256,256]{2,1,0:T(8,128)S(1)}, f32[2,256,256]{2,1,0:T(8,128)S(1)}, u32[]{:S(2)}, u32[]{:S(2)}) collective-permute-start(f32[2,256,256]{2,1,0:T(8,128)S(1)} %add.12), channel_id=1, source_target_pairs={{0,1},{1,2},{2,3},{4,5},{5,6},{6,7},{8,9},{9,10},{10,11},{12,13},{... | collective-permute-start | bytes 1572872 | tf_op jit(solution)/shard_map/ppermute | solution.py:23
  78.0 0.3 collective-permute-done.9
  78.3 1.4 %collective-permute-done.8 = f32[64,256]{1,0:T(8,128)S(1)} collective-permute-done((f32[64,256]{1,0:T(8,128)S(1)}, f32[64,256]{1,0:T(8,128)S(1)}, u32[]{:S(2)}, u32[]{:S(2)}) %collective-permute-start.8) | collective-permute-done | bytes 65568 | tf_op jit(solution)/shard_map/ppermute | solution.py:419
  79.8 10.8 %all-gather = f32[512,256]{1,0:T(8,128)S(1)} all-gather(f32[64,256]{1,0:T(8,128)S(1)} %add_add_fusion), channel_id=2, replica_groups=mesh['row'=8,'col'=4] {'row'}, dimensions={0}, use_global_device_ids=true | all-gather | bytes 589824 | tf_op jit(solution)/shard_map/all_gather | solution.py:488
  90.5 0.8 broadcast_multiply_fusion
  91.4 2.5 %first_merge.1.own_in = f32[2,512,512]{2,1,0:T(8,128)} custom-call(f32[2,512,512]{2,1,0:T(8,128)} %get-tuple-element.34.own_in, f32[2,256,512]{2,1,0:T(8,128)S(1)} %collective-permute-done.6.refs_0_, f32[2,256,256]{2,1,0:T(8,128)S(1)} %collective-permute-done.5.refs_1_), custom_call_target="tpu_custom_call", output_to_operand_aliasing={{}: (0, {})} | custom-call | tf_op jit(solution)/shard_map/first_merge/pallas_call | solution.py:285
  93.9 1.9 %last_merge.1 = f32[2,512,512]{2,1,0:T(8,128)} custom-call(f32[2,512,512]{2,1,0:T(8,128)} %first_merge.1.own_in, f32[2,256,256]{2,1,0:T(8,128)S(1)} %collective-permute-done.7.refs_0_), custom_call_target="tpu_custom_call", output_to_operand_aliasing={{}: (0, {})} | custom-call | tf_op jit(solution)/shard_map/last_merge/pallas_call | solution.py:285
  (27 shorter events, 0.1 us)
Async XLA Ops:
  0.6 7.1 %copy-start = (f32[2,512,512]{2,1,0:T(8,128)S(1)}, f32[2,512,512]{2,1,0:T(8,128)}, u32[]{:S(2)}) copy-start(f32[2,512,512]{2,1,0:T(8,128)} %tile_in.7) | copy-start | bytes 6291460
  0.6 7.0 %copy-start.11 = (s32[16,2]{0,1:T(2,128)S(1)}, s32[16,2]{0,1:T(2,128)}, u32[]{:S(2)}) copy-start(s32[16,2]{0,1:T(2,128)} %param.10) | copy-start | bytes 388
  0.7 7.1 %copy-start.9 = (s32[32]{0:T(128)S(1)}, s32[32]{0:T(128)}, u32[]{:S(2)}) copy-start(s32[32]{0:T(128)} %counts.5) | copy-start | bytes 388
  3.7 20.3 %collective-permute-start = (f32[2,256,512]{2,1,0:T(8,128)}, f32[2,256,512]{2,1,0:T(8,128)S(1)}, u32[]{:S(2)}, u32[]{:S(2)}) collective-permute-start(f32[2,256,512]{2,1,0:T(8,128)} %get-tuple-element.23), channel_id=1, source_target_pairs={{4,0},{8,4},{12,8},{16,12},{20,16},{24,20},{28,24},{5,1},{9,5},{13... | collective-permute-start | bytes 3145736 | tf_op jit(solution)/shard_map/ppermute | solution.py:23
  5.0 17.7 %collective-permute-start.1 = (f32[2,256,256]{2,1,0:T(8,128)}, f32[2,256,256]{2,1,0:T(8,128)}, u32[]{:S(2)}, u32[]{:S(2)}) collective-permute-start(f32[2,256,256]{2,1,0:T(8,128)} %get-tuple-element.24), channel_id=1, source_target_pairs={{1,0},{2,1},{3,2},{5,4},{6,5},{7,6},{9,8},{10,9},{11,10},{13,12},{... | collective-permute-start | bytes 1572872 | tf_op jit(solution)/shard_map/ppermute | solution.py:23
  6.3 27.6 %collective-permute-start.2 = (f32[2,256,256]{2,1,0:T(8,128)}, f32[2,256,256]{2,1,0:T(8,128)}, u32[]{:S(2)}, u32[]{:S(2)}) collective-permute-start(f32[2,256,256]{2,1,0:T(8,128)} %get-tuple-element.27), channel_id=1, source_target_pairs={{1,0},{2,1},{3,2},{5,4},{6,5},{7,6},{9,8},{10,9},{11,10},{13,12},{... | collective-permute-start | bytes 1572872 | tf_op jit(solution)/shard_map/ppermute | solution.py:23
  7.7 1.6 %copy-start.1 = (bf16[16,256,256]{2,1,0:T(8,128)(2,1)S(1)}, bf16[16,256,256]{2,1,0:T(8,128)(2,1)}, u32[]{:S(2)}) copy-start(bf16[16,256,256]{2,1,0:T(8,128)(2,1)} %amplitude.5) | copy-start | bytes 6291460
  9.3 1.0 %copy-start.3 = (f32[2,256,256]{2,1,0:T(8,128)S(1)}, f32[2,256,256]{2,1,0:T(8,128)}, u32[]{:S(2)}) copy-start(f32[2,256,256]{2,1,0:T(8,128)} %probe.5) | copy-start | bytes 1572868
  10.3 1.0 %copy-start.5 = (bf16[512,512]{1,0:T(8,128)(2,1)S(1)}, bf16[512,512]{1,0:T(8,128)(2,1)}, u32[]{:S(2)}) copy-start(bf16[512,512]{1,0:T(8,128)(2,1)} %constant.9.clone.inverse) | copy-start | bytes 1572868
  11.4 1.0 %copy-start.7 = (bf16[512,512]{1,0:T(8,128)(2,1)S(1)}, bf16[512,512]{1,0:T(8,128)(2,1)}, u32[]{:S(2)}) copy-start(bf16[512,512]{1,0:T(8,128)(2,1)} %constant.8.clone.forward) | copy-start | bytes 1572868
  12.4 11.5 %copy-start.2 = (bf16[16,256,256]{2,1,0:T(8,128)(2,1)S(1)}, bf16[16,256,256]{2,1,0:T(8,128)(2,1)}, u32[]{:S(2)}) copy-start(bf16[16,256,256]{2,1,0:T(8,128)(2,1)} %amplitude.5) | copy-start | bytes 6291460
  12.4 11.6 %copy-start.4 = (f32[2,256,256]{2,1,0:T(8,128)S(1)}, f32[2,256,256]{2,1,0:T(8,128)}, u32[]{:S(2)}) copy-start(f32[2,256,256]{2,1,0:T(8,128)} %probe.5) | copy-start | bytes 1572868
  12.4 11.6 %copy-start.6 = (bf16[512,512]{1,0:T(8,128)(2,1)S(1)}, bf16[512,512]{1,0:T(8,128)(2,1)}, u32[]{:S(2)}) copy-start(bf16[512,512]{1,0:T(8,128)(2,1)} %constant.9.clone.inverse) | copy-start | bytes 1572868
  18.5 1.3 %copy-start.10 = (f32[2,4,512,128]{3,2,1,0:T(8,128)}, f32[2,4,512,128]{3,2,1,0:T(8,128)S(1)}, u32[]{:S(2)}) copy-start(f32[2,4,512,128]{3,2,1,0:T(8,128)S(1)} %get-tuple-element.28.part) | copy-start | bytes 6291460
  22.7 11.2 %collective-permute-start.3 = (f32[2,256,256]{2,1,0:T(8,128)}, f32[2,256,256]{2,1,0:T(8,128)S(1)}, u32[]{:S(2)}, u32[]{:S(2)}) collective-permute-start(f32[2,256,256]{2,1,0:T(8,128)} %collective-permute-done.1.top_in), channel_id=1, source_target_pairs={{4,0},{8,4},{12,8},{16,12},{20,16},{24,20},{28,24},{5,1},{9,5},{13... | collective-permute-start | bytes 1572872 | tf_op jit(solution)/shard_map/ppermute | solution.py:23
  24.0 9.9 %copy-start.8 = (bf16[512,512]{1,0:T(8,128)(2,1)S(1)}, bf16[512,512]{1,0:T(8,128)(2,1)}, u32[]{:S(2)}) copy-start(bf16[512,512]{1,0:T(8,128)(2,1)} %constant.8.clone.forward) | copy-start | bytes 1572868
  43.5 22.1 %collective-permute-start.4 = (f32[2,256,256]{2,1,0:T(8,128)S(1)}, f32[2,256,256]{2,1,0:T(8,128)S(1)}, u32[]{:S(2)}, u32[]{:S(2)}) collective-permute-start(f32[2,256,256]{2,1,0:T(8,128)S(1)} %get-tuple-element.36), channel_id=1, source_target_pairs={{0,4},{4,8},{8,12},{12,16},{16,20},{20,24},{24,28},{1,5},{5,9},{9,... | collective-permute-start | bytes 1572872 | tf_op jit(solution)/shard_map/ppermute | solution.py:23
  44.9 20.8 %collective-permute-start.5 = (f32[2,256,256]{2,1,0:T(8,128)S(1)}, f32[2,256,256]{2,1,0:T(8,128)S(1)}, u32[]{:S(2)}, u32[]{:S(2)}) collective-permute-start(f32[2,256,256]{2,1,0:T(8,128)S(1)} %get-tuple-element.37), channel_id=1, source_target_pairs={{0,1},{1,2},{2,3},{4,5},{5,6},{6,7},{8,9},{9,10},{10,11},{12,13},{... | collective-permute-start | bytes 1572872 | tf_op jit(solution)/shard_map/ppermute | solution.py:23
  65.6 25.7 %collective-permute-start.6 = (f32[2,256,512]{2,1,0:T(8,128)}, f32[2,256,512]{2,1,0:T(8,128)S(1)}, u32[]{:S(2)}, u32[]{:S(2)}) collective-permute-start(f32[2,256,512]{2,1,0:T(8,128)} %get-tuple-element.39), channel_id=1, source_target_pairs={{0,4},{4,8},{8,12},{12,16},{16,20},{20,24},{24,28},{1,5},{5,9},{9,... | collective-permute-start | bytes 3145736 | tf_op jit(solution)/shard_map/ppermute | solution.py:23
  67.0 11.0 %collective-permute-start.10 = (f32[64,256]{1,0:T(8,128)S(1)}, f32[64,256]{1,0:T(8,128)S(1)}, u32[]{:S(2)}, u32[]{:S(2)}) collective-permute-start(f32[64,256]{1,0:T(8,128)S(1)} %reduce_sum.9), channel_id=1, source_target_pairs={{0,3},{1,2},{2,1},{3,0},{4,7},{5,6},{6,5},{7,4},{8,11},{9,10},{10,... | collective-permute-start | bytes 196616 | tf_op jit(solution)/shard_map/ppermute | solution.py:419
  73.0 5.4 %collective-permute-start.9 = (f32[64,256]{1,0:T(8,128)S(1)}, f32[64,256]{1,0:T(8,128)S(1)}, u32[]{:S(2)}, u32[]{:S(2)}) collective-permute-start(f32[64,256]{1,0:T(8,128)S(1)} %reduce_sum.9), channel_id=1, source_target_pairs={{0,2},{1,3},{2,0},{3,1},{4,6},{5,7},{6,4},{7,5},{8,10},{9,11},{10,... | collective-permute-start | bytes 196616 | tf_op jit(solution)/shard_map/ppermute | solution.py:419
  74.0 5.8 %collective-permute-start.8 = (f32[64,256]{1,0:T(8,128)S(1)}, f32[64,256]{1,0:T(8,128)S(1)}, u32[]{:S(2)}, u32[]{:S(2)}) collective-permute-start(f32[64,256]{1,0:T(8,128)S(1)} %reduce_sum.9), channel_id=1, source_target_pairs={{0,1},{1,0},{2,3},{3,2},{4,5},{5,4},{6,7},{7,6},{8,9},{9,8},{10,11... | collective-permute-start | bytes 196616 | tf_op jit(solution)/shard_map/ppermute | solution.py:419
  74.5 19.4 %collective-permute-start.7 = (f32[2,256,256]{2,1,0:T(8,128)S(1)}, f32[2,256,256]{2,1,0:T(8,128)S(1)}, u32[]{:S(2)}, u32[]{:S(2)}) collective-permute-start(f32[2,256,256]{2,1,0:T(8,128)S(1)} %add.12), channel_id=1, source_target_pairs={{0,1},{1,2},{2,3},{4,5},{5,6},{6,7},{8,9},{9,10},{10,11},{12,13},{... | collective-permute-start | bytes 1572872 | tf_op jit(solution)/shard_map/ppermute | solution.py:23
